TPU v7x, 32 devices: a whole 2x2x4 slice. The times are simulated.
32 devices in a mesh: row: 4 (over x, core), col: 8 (over z, y).
Axes of the slice: x: 2, y: 2, z: 4, core: 2. Of those that a mesh axis runs over, the one named last changes fastest.
Arguments:
- left_image: bfloat16 [64, 1024], P('row', 'col'), may hold values from -32 to 32, as said below
- right_image: bfloat16 [64, 1024], P('row', 'col'), may hold values from -32 to 32, as said below
- kernel_one: float32 [64, 9], replicated, may hold values from -2 to 2
- bias_one: float32 [64], replicated, may hold values from -1.5 to 1.5
- kernel_two: bfloat16 [9, 64, 64], replicated, may hold values from -0.25 to 0.25
- bias_two: float32 [64], replicated, may hold values from -1.5 to 1.5
- kernel_three: bfloat16 [9, 64, 64], replicated, may hold values from -0.25 to 0.25
- bias_three: float32 [64], replicated, may hold values from -1.5 to 1.5
- block_list: int32 [4, 8, 8], P('row', 'col'), may hold values from 0 to 15, as said below
- block_count: int32 [4, 8], P('row', 'col'), may hold values from 1 to 8, as said below
Outputs:
- disparity: float32 [64, 1024], P('row', 'col')
Inputs may be any that keep to these rules, and one draw needn't show every extreme that they name: `left_image`: pixel values. `right_image`: pixel values. `block_list`: in each tile the first block_count entries are distinct and ascending; later entries have no meaning. `block_count`: some tile lists 8 blocks.
All inputs are finite; a program needn't handle non-finite values.
Results may differ from a plain program's by a relative error of at most 0.0025.
The roundings to bfloat16 on the way count: a program that leaves them out, or rounds other values in their place, can miss the bound.
Values may be sent and summed in bfloat16 or wider, within the bound.
No kernel may reach another device: no remote copies, remote signals or barrier semaphores. Data moves between devices by JAX's collectives and lax.ppermute only.
A program may use at most 64 MiB of HBM per device.

v0:
```python
import functools
import math

import jax
import jax.numpy as jnp
from jax import lax
from jax.experimental import pallas as pl
from jax.experimental.pallas import tpu as pltpu
from jax.sharding import PartitionSpec as P

DBLOCK = 64
SPAN = 4
SEGS = 16
PAD = 8
NT = (((1,), (1,)), ((), ()))
TN = (((0,), (0,)), ((), ()))
F32 = jnp.float32
BF16 = jnp.bfloat16


def iota(shape, dim):
    return lax.broadcasted_iota(jnp.int32, shape, dim)


class Plan:
    def __init__(self, mesh, rows, cols, chans):
        self.n_row, self.n_col = mesh.shape["row"], mesh.shape["col"]
        self.rows, self.cols, self.chans = rows, cols, chans
        self.ring = self.n_col == 2 * SPAN
        self.tiles = self.n_col if self.ring else 16
        self.width = self.n_col * cols
        self.seg = self.tiles * cols // SEGS
        self.quads = self.seg // 2
        self.seg_left = cols // SEGS
        self.quads_left = self.seg_left // 2
        self.left_at = (self.quads + 2) * SEGS
        self.total = self.left_at + (self.quads_left + 2) * SEGS
        self.points = self.quads * SEGS
        self.lanes = 4 * chans


def prep_kernel(plan, k1_ref, k2_ref, k3_ref, place_ref, list_ref, w1_ref, w2_ref, w3_ref, bias_ref, disp_ref):
    ch = plan.chans
    kernel = k1_ref[...]
    high = kernel.astype(BF16)
    rest = kernel - high.astype(F32)
    middle = rest.astype(BF16)
    low = (rest - middle.astype(F32)).astype(BF16)
    taps = kernel.shape[1]
    w1_ref[...] = jnp.zeros(w1_ref.shape, BF16)
    for part, values in enumerate((high, middle, low)):
        for out in range(4):
            oy, ox = divmod(out, 2)
            row, tap = iota((5 * 64, taps), 0), iota((5 * 64, taps), 1)
            step, px, y = row // 64, (row // 16) % 4, row % 16
            pick = (px == tap % 3 + ox) & (y == 2 * step + oy + tap // 3)
            block = lax.dot_general(
                jnp.where(pick, 1.0, 0.0).astype(BF16), values, NT, preferred_element_type=F32
            ).astype(BF16)
            for step in range(5):
                w1_ref[step, part * 64 : part * 64 + 64, out * ch : out * ch + ch] = block[
                    step * 64 : step * 64 + 64
                ]
    for source, target in ((k2_ref, w2_ref), (k3_ref, w3_ref)):
        turned = [source[tap].astype(F32).T for tap in range(9)]
        nothing = jnp.zeros((ch, ch), F32)
        for py in range(4):
            for px in range(4):
                pieces = []
                for out in range(4):
                    ty, tx = py - out // 2, px - out % 2
                    inside = 0 <= ty < 3 and 0 <= tx < 3
                    pieces.append(turned[3 * ty + tx] if inside else nothing)
                quad, sub = (py // 2) * 2 + px // 2, (py % 2) * 2 + px % 2
                target[quad, sub * ch : sub * ch + ch, :] = jnp.concatenate(pieces, axis=1).astype(BF16)
    col = place_ref[1]
    bits = jnp.int32(0)
    for k in range(list_ref.shape[0]):
        bits = bits | jnp.where(k < place_ref[2], jnp.left_shift(jnp.int32(1), list_ref[k]), 0)
    reach = SPAN * plan.cols
    shape = (plan.points, 4 * SEGS * plan.quads_left)
    m, n = iota(shape, 0), iota(shape, 1)
    per = SEGS * plan.quads_left
    q = (m % SEGS) * plan.seg + 2 * (m // SEGS) + n // (2 * per)
    left = n % per
    p = (left % SEGS) * plan.seg_left + 2 * (left // SEGS) + (n // per) % 2
    if plan.ring:
        d = col * plan.cols + p - q
        d = jnp.where(d < -reach, d + plan.width, d)
        d = jnp.where(d >= reach, d - plan.width, d)
        listed = jnp.right_shift(bits, (d + reach) // DBLOCK) & 1
    else:
        d = 5 * plan.cols + p - q
        inside = (d >= -reach) & (d < reach)
        block = jnp.where(inside, (d + reach) // DBLOCK, 31)
        listed = jnp.where(inside, jnp.right_shift(bits, block) & 1, 0)
    bias_ref[...] = jnp.where(listed > 0, 0.0, -1e30).astype(F32)
    disp_ref[...] = d.astype(F32)


def main_kernel(
    plan, place_ref, g_ref, w1_ref, b_ref, w2_ref, w3_ref, bias_ref, disp_ref, out_ref,
    ext_ref, extl_ref, f_ref, x1_ref, x2_ref, x3_ref, lb_ref, s_ref, tot_ref, mom_ref,
):
    rows, cols, ch = plan.rows, plan.cols, plan.chans
    row, col = place_ref[0], place_ref[1]
    first_row, last_row = row == 0, row == plan.n_row - 1

    shape = (3 * rows, 512)
    v, lane = iota(shape, 0), iota(shape, 1)
    y = 10 * (lane // 256) + lane % 16
    keep = (v == rows - 3 + y) & (y < rows + 6) & (lane % 256 < 192)
    keep = keep & ((v >= rows) | jnp.logical_not(first_row))
    keep = keep & ((v < 2 * rows) | jnp.logical_not(last_row))
    spread = jnp.where(keep, 1.0, 0.0).astype(BF16)

    def fetch(image, tile):
        parts = []
        for dr in (-1, 0, 1):
            at = jnp.clip(row + dr, 0, plan.n_row - 1) * plan.n_col + tile
            parts.append(g_ref[at, image])
        return lax.dot_general(
            jnp.concatenate(parts, axis=0), spread, TN, preferred_element_type=F32
        )

    for t in range(plan.tiles):
        tile = t if plan.ring else lax.rem(col + (t - 5 + plan.n_col), plan.n_col)
        value = fetch(1, tile)
        for k in range(4):
            ext_ref[k, PAD + t * cols : PAD + (t + 1) * cols, :] = value[:, 128 * k : 128 * k + 128]
    for k in range(4):
        ext_ref[k, 0:PAD, :] = jnp.zeros((PAD, 128), F32)
        ext_ref[k, PAD + plan.tiles * cols :, :] = jnp.zeros((PAD, 128), F32)
    for t in range(3):
        tile = lax.rem(col + (t - 1 + plan.n_col), plan.n_col)
        value = fetch(0, tile)
        for k in range(4):
            extl_ref[k, t * cols : (t + 1) * cols, :] = value[:, 128 * k : 128 * k + 128]

    seg_id = iota((SEGS, 1), 0)
    if plan.ring:
        begin = seg_id * plan.seg
    else:
        begin = lax.rem((col + plan.n_col - 5) * cols + seg_id * plan.seg, plan.width)
    edges_right = (
        jnp.where(begin == 0, 0.0, 1.0).astype(F32),
        jnp.where(begin + plan.seg == plan.width, 0.0, 1.0).astype(F32),
    )
    edges_left = (
        jnp.where((col == 0) & (seg_id == 0), 0.0, 1.0).astype(F32),
        jnp.where((col == plan.n_col - 1) & (seg_id == SEGS - 1), 0.0, 1.0).astype(F32),
    )
    areas = (
        (ext_ref, PAD, plan.seg, 0, edges_right),
        (extl_ref, cols, plan.seg_left, plan.left_at, edges_left),
    )
    px_lane = (iota((SEGS, 128), 1) // 16) % 4
    for half in range(2):
        for source, pad, seg, at, edges in areas:
            for c in range(seg // 2 + 2):
                groups = []
                for k in range(2):
                    value = None
                    for px in range(4):
                        x = 2 * c + px - 3
                        piece = source[2 * half + k, pl.ds(pad + x, SEGS, stride=seg), :]
                        if x < 0:
                            piece = piece * edges[0]
                        if x >= seg:
                            piece = piece * edges[1]
                        value = piece if value is None else jnp.where(px_lane == px, piece, value)
                    groups.append(value)
                f_ref[half, at + c * SEGS : at + (c + 1) * SEGS, :] = jnp.concatenate(
                    groups, axis=1
                ).astype(BF16)

    def clear_first(value):
        pieces = []
        for _, _, seg, at, edges in areas:
            end = at + (seg // 2 + 2) * SEGS
            pieces.append(value[at : at + SEGS] * edges[0])
            pieces.append(value[at + SEGS : end - SEGS])
            pieces.append(value[end - SEGS : end] * edges[1])
        return jnp.concatenate(pieces, axis=0)

    for half in range(2):
        def layer_one(step, carry):
            value = jnp.dot(f_ref[half], w1_ref[step], preferred_element_type=F32)
            value = jax.nn.relu(value + b_ref[0:1, :])
            x1_ref[5 * half + step] = clear_first(value).astype(BF16)
            return carry

        lax.fori_loop(0, 5, layer_one, 0)

    @pl.when(first_row)
    def _():
        x1_ref[0] = jnp.zeros(x1_ref.shape[1:], BF16)

    @pl.when(last_row)
    def _():
        x1_ref[9] = jnp.zeros(x1_ref.shape[1:], BF16)

    def four(source, weight, r, count):
        value = jnp.dot(source[r, 0:count], weight[0], preferred_element_type=F32)
        value += jnp.dot(source[r, SEGS : count + SEGS], weight[1], preferred_element_type=F32)
        value += jnp.dot(source[r + 1, 0:count], weight[2], preferred_element_type=F32)
        return value + jnp.dot(source[r + 1, SEGS : count + SEGS], weight[3], preferred_element_type=F32)

    count_two = plan.total - SEGS
    odd = (iota((SEGS, plan.lanes), 1) // ch) % 2

    def layer_two(r, carry):
        value = jax.nn.relu(four(x1_ref, w2_ref, r, count_two) + b_ref[1:2, :])
        x2_ref[r] = value.astype(BF16)
        for _, _, seg, at, edges in areas:
            end = at + (seg // 2 + 1) * SEGS
            head = value[at : at + SEGS]
            x2_ref[r, at : at + SEGS] = jnp.where(odd == 0, head * edges[0], head).astype(BF16)
            tail = value[end - SEGS : end]
            x2_ref[r, end - SEGS : end] = jnp.where(odd == 1, tail * edges[1], tail).astype(BF16)
        return carry

    lax.fori_loop(0, 9, layer_two, 0)

    @pl.when(first_row)
    def _():
        x2_ref[0, :, 0 : 2 * ch] = jnp.zeros((count_two, 2 * ch), BF16)

    @pl.when(last_row)
    def _():
        x2_ref[8, :, 2 * ch :] = jnp.zeros((count_two, 2 * ch), BF16)

    count_three = count_two - SEGS
    per = plan.quads_left * SEGS
    group = iota((per, plan.lanes), 1) // ch

    def layer_three(r, carry):
        value = four(x2_ref, w3_ref, r, count_three) + b_ref[2:3, :]
        x3_ref[r] = value[: plan.points].astype(BF16)
        left = value[plan.left_at : plan.left_at + per]
        swapped = jnp.concatenate(
            [left[:, ch : 2 * ch], left[:, :ch], left[:, 3 * ch :], left[:, 2 * ch : 3 * ch]], axis=1
        )
        for dy in range(2):
            for dxr in range(2):
                for dxl in range(2):
                    block = jnp.where(group == 2 * dy + dxr, left if dxl == dxr else swapped, 0.0)
                    at = (4 * dy + 2 * dxr + dxl) * per
                    lb_ref[r, at : at + per] = block.astype(BF16)
        return carry

    lax.fori_loop(0, 8, layer_three, 0)

    scale = math.log2(math.e) / math.sqrt(ch)
    pair = 2 * per

    def score(r, carry):
        s_ref[...] = lax.dot_general(x3_ref[r], lb_ref[r], NT, preferred_element_type=F32)
        for dy in range(2):
            lanes = slice(dy * 2 * pair, (dy + 1) * 2 * pair)

            def find_top(i, top):
                at = pl.ds(pl.multiple_of(i * 32, 32), 32)
                value = s_ref[at, lanes] + bias_ref[at, :]
                s_ref[at, lanes] = value
                return jnp.maximum(top, jnp.max(value.reshape(4, 8, 2 * pair), axis=0))

            top = lax.fori_loop(
                0, plan.points // 32, find_top, jnp.full((8, 2 * pair), -1e30, F32), unroll=4
            )
            top = jnp.max(top, axis=0, keepdims=True)
            top = jnp.maximum(top[:, :pair], top[:, pair:])
            top = jnp.broadcast_to(jnp.concatenate([top, top], axis=1), (8, 2 * pair))

            def add_up(i, state):
                total, moment = state
                at = pl.ds(pl.multiple_of(i * 32, 32), 32)
                value = s_ref[at, lanes].reshape(4, 8, 2 * pair) - top[None]
                weight = jnp.exp2(value * scale)
                total = total + jnp.sum(weight, axis=0)
                moment = moment + jnp.sum(weight * disp_ref[at, :].reshape(4, 8, 2 * pair), axis=0)
                return total, moment

            zero = jnp.zeros((8, 2 * pair), F32)
            total, moment = lax.fori_loop(0, plan.points // 32, add_up, (zero, zero), unroll=4)
            total = jnp.sum(total, axis=0, keepdims=True)
            moment = jnp.sum(moment, axis=0, keepdims=True)
            tot_ref[pl.ds(2 * r + dy, 1), :] = total[:, :pair] + total[:, pair:]
            mom_ref[pl.ds(2 * r + dy, 1), :] = moment[:, :pair] + moment[:, pair:]
        return carry

    lax.fori_loop(0, 8, score, 0)

    n, p = iota((pair, cols), 0), iota((pair, cols), 1)
    left = n % per
    place = (left % SEGS) * plan.seg_left + 2 * (left // SEGS) + n // per
    turn = jnp.where(place == p, 1.0, 0.0).astype(F32)
    value = mom_ref[...] / tot_ref[...] * (1.0 / cols)
    out_ref[...] = jnp.dot(value, turn, precision=lax.Precision.HIGHEST, preferred_element_type=F32)


def solution(mesh):
    def per_device(
        left_image, right_image, kernel_one, bias_one, kernel_two, bias_two,
        kernel_three, bias_three, block_list, block_count,
    ):
        rows, cols = left_image.shape
        ch = kernel_one.shape[0]
        plan = Plan(mesh, rows, cols, ch)
        devices = plan.n_row * plan.n_col
        images = jnp.stack([left_image, right_image])
        gathered = lax.all_to_all(
            jnp.broadcast_to(images, (devices,) + images.shape), ("row", "col"), 0, 0
        )
        place = jnp.stack(
            [lax.axis_index("row"), lax.axis_index("col"), block_count[0, 0]]
        ).astype(jnp.int32)
        vmem = pl.BlockSpec(memory_space=pltpu.VMEM)
        smem = pl.BlockSpec(memory_space=pltpu.SMEM)
        lanes = plan.lanes
        n_left = 4 * SEGS * plan.quads_left
        w1, w2, w3, mask, disp = pl.pallas_call(
            functools.partial(prep_kernel, plan),
            out_shape=(
                jax.ShapeDtypeStruct((5, 256, lanes), BF16),
                jax.ShapeDtypeStruct((4, lanes, lanes), BF16),
                jax.ShapeDtypeStruct((4, lanes, lanes), BF16),
                jax.ShapeDtypeStruct((plan.points, n_left), F32),
                jax.ShapeDtypeStruct((plan.points, n_left), F32),
            ),
            in_specs=[vmem, vmem, vmem, smem, smem],
            out_specs=(vmem,) * 5,
            compiler_params=pltpu.CompilerParams(vmem_limit_bytes=48 * 2**20),
        )(kernel_one, kernel_two, kernel_three, place, block_list.reshape(-1))
        biases = jnp.stack([jnp.tile(b, 4) for b in (bias_one, bias_two, bias_three)])
        return pl.pallas_call(
            functools.partial(main_kernel, plan),
            out_shape=jax.ShapeDtypeStruct((rows, cols), F32),
            in_specs=[smem] + [vmem] * 7,
            out_specs=vmem,
            scratch_shapes=[
                pltpu.VMEM((4, plan.tiles * cols + 2 * PAD, 128), F32),
                pltpu.VMEM((4, 3 * cols, 128), F32),
                pltpu.VMEM((2, plan.total, 256), BF16),
                pltpu.VMEM((10, plan.total, lanes), BF16),
                pltpu.VMEM((9, plan.total - SEGS, lanes), BF16),
                pltpu.VMEM((8, plan.points, lanes), BF16),
                pltpu.VMEM((8, 2 * n_left, lanes), BF16),
                pltpu.VMEM((plan.points, 2 * n_left), F32),
                pltpu.VMEM((rows, cols), F32),
                pltpu.VMEM((rows, cols), F32),
            ],
            compiler_params=pltpu.CompilerParams(vmem_limit_bytes=56 * 2**20),
        )(place, gathered, w1, biases, w2, w3, mask, disp)

    return jax.shard_map(
        per_device,
        mesh=mesh,
        in_specs=(
            P("row", "col"), P("row", "col"), P(), P(), P(), P(), P(), P(),
            P("row", "col", None), P("row", "col"),
        ),
        out_specs=P("row", "col"),
        check_vma=False,
    )
```

profile of v0, /device:TPU:0, one launch (start us, length us, event | category | flops | bytes accessed | tf_op | source)
XLA Modules:
  0.0 43.3 jit_solution(16761410613358335843)
XLA Ops:
  0.0 0.7 %pad_maximum_fusion = bf16[2,16,128]{2,1,0:T(8,128)(2,1)S(1)} fusion(bf16[1,16,128]{2,1,0:T(8,128)(2,1)} %bitcast.8, bf16[1,16,128]{2,1,0:T(8,128)(2,1)} %bitcast.9), kind=kLoop, calls=%fused_computation | loop fusion | flops 4096 | bytes 16384 | tf_op jit(solution)/shard_map/stack | solution.py:311
  0.7 0.7 %broadcast_in_dim.3 = bf16[32,2,16,128]{3,2,1,0:T(8,128)(2,1)} broadcast(bf16[2,16,128]{2,1,0:T(8,128)(2,1)S(1)} %pad_maximum_fusion), dimensions={1,2,3} | broadcast | bytes 270336 | tf_op jit(solution)/shard_map/broadcast_in_dim | solution.py:313
  1.5 0.0 copy-start.5
  1.5 0.0 copy-start.6
  1.5 7.3 %all-to-all-start = ((bf16[32,2,16,128]{3,2,1,0:T(8,128)(2,1)}), bf16[32,2,16,128]{3,2,1,0:T(8,128)(2,1)S(1)}, u32[]{:S(2)}, u32[]{:S(2)}) async-start(bf16[32,2,16,128]{3,2,1,0:T(8,128)(2,1)} %broadcast_in_dim.3), calls=%async_computation | async-start | bytes 524288 | tf_op jit(solution)/shard_map/all_to_all | solution.py:312
  8.8 0.0 copy-start.10
  9.4 0.0 copy-done.10
  9.5 0.0 copy-start.11
  9.5 0.1 copy.11.k1_ref
  9.6 0.6 %copy-done.11 = f32[64]{0:T(128)S(1)} copy-done((f32[64]{0:T(128)S(1)}, f32[64]{0:T(128)}, u32[]{:S(2)}) %copy-start.11) | copy-done | bytes 280
  10.1 0.0 copy-start.12
  10.1 0.1 stack_tile.11
  10.2 0.6 %copy-done.12 = f32[64]{0:T(128)S(1)} copy-done((f32[64]{0:T(128)S(1)}, f32[64]{0:T(128)}, u32[]{:S(2)}) %copy-start.12) | copy-done | bytes 280
  10.8 0.0 copy-start.13
  10.8 0.1 stack_tile.10
  10.9 0.6 %copy-done.13 = f32[64]{0:T(128)S(1)} copy-done((f32[64]{0:T(128)S(1)}, f32[64]{0:T(128)}, u32[]{:S(2)}) %copy-start.13) | copy-done | bytes 280
  11.4 0.1 stack_tile.9
  11.5 0.1 pad_add_fusion.place_ref
  11.6 0.0 copy-start.7
  11.6 0.0 copy-start.8
  11.6 0.6 %copy-done.7 = s32[3]{0:T(128)} copy-done((s32[3]{0:T(128)}, s32[3]{0:T(128)S(1)}, u32[]{:S(2)}) %copy-start.7) | copy-done | bytes 36
  12.2 0.0 copy-done.5
  12.2 0.0 copy-done.6
  12.2 0.1 copy-done.8
  12.3 1.9 %shard_map.100 = (bf16[5,256,256]{2,1,0:T(8,128)(2,1)S(1)}, bf16[4,256,256]{2,1,0:T(8,128)(2,1)S(1)}, bf16[4,256,256]{2,1,0:T(8,128)(2,1)S(1)}, f32[512,256]{1,0:T(8,128)S(1)}, f32[512,256]{1,0:T(8,128)S(1)}) custom-call(f32[64,9]{1,0:T(8,128)S(1)} %copy.11.k1_ref, bf16[9,64,64]{2,1,0:T(8,128)(2,1)S(1)} %copy-done.5, bf16[9,64,64]{2,1,0:T(8,128)(2,1)S(1)} %copy-done.6, ...), custom_call_target="tpu_custom_call" | custom-call | tf_op jit(solution)/shard_map/pallas_call | solution.py:322
  14.1 0.0 copy-start
  14.1 0.8 %copy-done = bf16[5,256,256]{2,1,0:T(8,128)(2,1)} copy-done((bf16[5,256,256]{2,1,0:T(8,128)(2,1)}, bf16[5,256,256]{2,1,0:T(8,128)(2,1)S(1)}, u32[]{:S(2)}) %copy-start) | copy-done | bytes 655384
  15.0 0.0 copy-start.1
  15.0 0.8 %copy-done.1 = bf16[4,256,256]{2,1,0:T(8,128)(2,1)} copy-done((bf16[4,256,256]{2,1,0:T(8,128)(2,1)}, bf16[4,256,256]{2,1,0:T(8,128)(2,1)S(1)}, u32[]{:S(2)}) %copy-start.1) | copy-done | bytes 524312
  15.8 0.0 copy-start.2
  15.8 0.8 %copy-done.2 = bf16[4,256,256]{2,1,0:T(8,128)(2,1)} copy-done((bf16[4,256,256]{2,1,0:T(8,128)(2,1)}, bf16[4,256,256]{2,1,0:T(8,128)(2,1)S(1)}, u32[]{:S(2)}) %copy-start.2) | copy-done | bytes 524312
  16.6 0.0 copy-start.3
  16.6 0.8 %copy-done.3 = f32[512,256]{1,0:T(8,128)} copy-done((f32[512,256]{1,0:T(8,128)}, f32[512,256]{1,0:T(8,128)S(1)}, u32[]{:S(2)}) %copy-start.3) | copy-done | bytes 524312
  17.4 0.0 copy-start.4
  17.4 0.8 %copy-done.4 = f32[512,256]{1,0:T(8,128)} copy-done((f32[512,256]{1,0:T(8,128)}, f32[512,256]{1,0:T(8,128)S(1)}, u32[]{:S(2)}) %copy-start.4) | copy-done | bytes 524312
  18.2 0.6 %pad_maximum_fusion.1.b_ref = f32[3,256]{1,0:T(4,128)} fusion(f32[1,256]{1,0:T(1,128)S(1)} %stack_tile.11, f32[1,256]{1,0:T(1,128)S(1)} %stack_tile.10, f32[1,256]{1,0:T(1,128)S(1)} %stack_tile.9), kind=kLoop, calls=%fused_computation.1 | loop fusion | flops 1536 | bytes 6144 | tf_op jit(solution)/shard_map/stack | solution.py:335
  18.8 0.7 %all-to-all-done.g_ref = bf16[32,2,16,128]{3,2,1,0:T(8,128)(2,1)S(1)} async-done(((bf16[32,2,16,128]{3,2,1,0:T(8,128)(2,1)}), bf16[32,2,16,128]{3,2,1,0:T(8,128)(2,1)S(1)}, u32[]{:S(2)}, u32[]{:S(2)}) %all-to-all-start) | async-done | bytes 262176 | tf_op jit(solution)/shard_map/all_to_all | solution.py:312
  19.4 0.0 copy-start.9
  19.4 0.7 %copy-done.9 = bf16[32,2,16,128]{3,2,1,0:T(8,128)(2,1)} copy-done((bf16[32,2,16,128]{3,2,1,0:T(8,128)(2,1)}, bf16[32,2,16,128]{3,2,1,0:T(8,128)(2,1)S(1)}, u32[]{:S(2)}) %copy-start.9) | copy-done | bytes 262168
  20.1 23.2 %shard_map.101 = f32[16,128]{1,0:T(8,128)} custom-call(s32[3]{0:T(128)} %copy-done.7, bf16[32,2,16,128]{3,2,1,0:T(8,128)(2,1)} %copy-done.9, bf16[5,256,256]{2,1,0:T(8,128)(2,1)} %copy-done, f32[3,256]{1,0:T(4,128)} %pad_maximum_fusion.1.b_ref, bf16[4,256,256]{2,1,0:T(8,128)(2,1)} %copy-done.1, bf16[4,256,256]{2,1,0:T(8,128)(2,1)} %copy-done.2, ...), custom_call_target="tpu_custom_call" | custom-call | tf_op jit(solution)/shard_map/pallas_call | solution.py:336
  (3 shorter events, 0.0 us)
Async XLA Ops:
  1.5 10.7 %copy-start.5 = (bf16[9,64,64]{2,1,0:T(8,128)(2,1)S(1)}, bf16[9,64,64]{2,1,0:T(8,128)(2,1)}, u32[]{:S(2)}) copy-start(bf16[9,64,64]{2,1,0:T(8,128)(2,1)} %k2_ref.1) | copy-start | bytes 221188
  1.5 10.7 %copy-start.6 = (bf16[9,64,64]{2,1,0:T(8,128)(2,1)S(1)}, bf16[9,64,64]{2,1,0:T(8,128)(2,1)}, u32[]{:S(2)}) copy-start(bf16[9,64,64]{2,1,0:T(8,128)(2,1)} %k3_ref.1) | copy-start | bytes 221188
  1.5 18.0 %all-to-all-start = ((bf16[32,2,16,128]{3,2,1,0:T(8,128)(2,1)}), bf16[32,2,16,128]{3,2,1,0:T(8,128)(2,1)S(1)}, u32[]{:S(2)}, u32[]{:S(2)}) async-start(bf16[32,2,16,128]{3,2,1,0:T(8,128)(2,1)} %broadcast_in_dim.3), calls=%async_computation | async-start | bytes 524288 | tf_op jit(solution)/shard_map/all_to_all | solution.py:312
  8.8 0.7 %copy-start.10 = (f32[64,9]{0,1:T(8,128)S(1)}, f32[64,9]{0,1:T(8,128)}, u32[]{:S(2)}) copy-start(f32[64,9]{0,1:T(8,128)} %param.12) | copy-start | bytes 6916
  9.5 0.7 %copy-start.11 = (f32[64]{0:T(128)S(1)}, f32[64]{0:T(128)}, u32[]{:S(2)}) copy-start(f32[64]{0:T(128)} %param.17) | copy-start | bytes 772
  10.1 0.7 %copy-start.12 = (f32[64]{0:T(128)S(1)}, f32[64]{0:T(128)}, u32[]{:S(2)}) copy-start(f32[64]{0:T(128)} %param.15) | copy-start | bytes 772
  10.8 0.7 %copy-start.13 = (f32[64]{0:T(128)S(1)}, f32[64]{0:T(128)}, u32[]{:S(2)}) copy-start(f32[64]{0:T(128)} %param.13) | copy-start | bytes 772
  11.6 0.6 %copy-start.7 = (s32[3]{0:T(128)}, s32[3]{0:T(128)S(1)}, u32[]{:S(2)}) copy-start(s32[3]{0:T(128)S(1)} %pad_add_fusion.place_ref) | copy-start | bytes 40
  11.6 0.7 %copy-start.8 = (s32[1,1,8]{2,1,0:T(1,128)S(1)}, s32[1,1,8]{2,1,0:T(1,128)}, u32[]{:S(2)}) copy-start(s32[1,1,8]{2,1,0:T(1,128)} %param.18) | copy-start | bytes 100
  14.1 0.8 %copy-start = (bf16[5,256,256]{2,1,0:T(8,128)(2,1)}, bf16[5,256,256]{2,1,0:T(8,128)(2,1)S(1)}, u32[]{:S(2)}) copy-start(bf16[5,256,256]{2,1,0:T(8,128)(2,1)S(1)} %get-tuple-element.10.w1_ref) | copy-start | bytes 1966084
  15.0 0.8 %copy-start.1 = (bf16[4,256,256]{2,1,0:T(8,128)(2,1)}, bf16[4,256,256]{2,1,0:T(8,128)(2,1)S(1)}, u32[]{:S(2)}) copy-start(bf16[4,256,256]{2,1,0:T(8,128)(2,1)S(1)} %get-tuple-element.11.w2_ref) | copy-start | bytes 1572868
  15.8 0.8 %copy-start.2 = (bf16[4,256,256]{2,1,0:T(8,128)(2,1)}, bf16[4,256,256]{2,1,0:T(8,128)(2,1)S(1)}, u32[]{:S(2)}) copy-start(bf16[4,256,256]{2,1,0:T(8,128)(2,1)S(1)} %get-tuple-element.12.w3_ref) | copy-start | bytes 1572868
  16.6 0.8 %copy-start.3 = (f32[512,256]{1,0:T(8,128)}, f32[512,256]{1,0:T(8,128)S(1)}, u32[]{:S(2)}) copy-start(f32[512,256]{1,0:T(8,128)S(1)} %get-tuple-element.13.bias_ref) | copy-start | bytes 1572868
  17.4 0.8 %copy-start.4 = (f32[512,256]{1,0:T(8,128)}, f32[512,256]{1,0:T(8,128)S(1)}, u32[]{:S(2)}) copy-start(f32[512,256]{1,0:T(8,128)S(1)} %get-tuple-element.14.disp_ref) | copy-start | bytes 1572868
  19.4 0.7 %copy-start.9 = (bf16[32,2,16,128]{3,2,1,0:T(8,128)(2,1)}, bf16[32,2,16,128]{3,2,1,0:T(8,128)(2,1)S(1)}, u32[]{:S(2)}) copy-start(bf16[32,2,16,128]{3,2,1,0:T(8,128)(2,1)S(1)} %all-to-all-done.g_ref) | copy-start | bytes 786436
where the time goes:
time: 43.7 us; the launch traced here: 43.3 us
  Pallas kernels  25.1 us (57%)
  local copies, waits for them, and re-layouts  8.25 us (19%)
  starting transfers between devices  7.3 us (17%)
  other arithmetic  1.36 us (3%)
  between operations  0.71 us (2%)
  waiting for transfers between devices  0.65 us (1%)
    pallas_call x1, Pallas kernels, per_device(): pl.pallas_call(functools.partial(main_kernel, plan), out_shape=jax.ShapeD...  23.2 us
    all_to_all x1, starting transfers between devices, per_device(): lax.all_to_all(jnp.broadcast_to(images, (devices,) + images.shape), ('row...  7.3 us
    unnamed x29, local copies, waits for them, and re-layouts  7.24 us
    pallas_call x1, Pallas kernels, per_device(): pl.pallas_call(functools.partial(prep_kernel, plan), out_shape=(jax.Shape...  1.86 us
  transfers between devices with their start and end apart: 1, of which 1 were waited for; matrix products, arithmetic and copies ran while one was open for 2% of the time, Pallas kernels for 4%

commit v1 on v0

--- a/solution.py
+++ b/solution.py
@@ -100,7 +100,7 @@
 
 def main_kernel(
     plan, place_ref, g_ref, w1_ref, b_ref, w2_ref, w3_ref, bias_ref, disp_ref, out_ref,
-    ext_ref, extl_ref, f_ref, x1_ref, x2_ref, x3_ref, lb_ref, s_ref, tot_ref, mom_ref,
+    v_ref, ext_ref, f_ref, x1_ref, x2_ref, x3_ref, lb_ref, s_ref, tot_ref, mom_ref,
 ):
     rows, cols, ch = plan.rows, plan.cols, plan.chans
     row, col = place_ref[0], place_ref[1]
@@ -114,28 +114,19 @@
     keep = keep & ((v < 2 * rows) | jnp.logical_not(last_row))
     spread = jnp.where(keep, 1.0, 0.0).astype(BF16)
 
-    def fetch(image, tile):
-        parts = []
-        for dr in (-1, 0, 1):
-            at = jnp.clip(row + dr, 0, plan.n_row - 1) * plan.n_col + tile
-            parts.append(g_ref[at, image])
-        return lax.dot_general(
-            jnp.concatenate(parts, axis=0), spread, TN, preferred_element_type=F32
-        )
-
-    for t in range(plan.tiles):
-        tile = t if plan.ring else lax.rem(col + (t - 5 + plan.n_col), plan.n_col)
-        value = fetch(1, tile)
-        for k in range(4):
-            ext_ref[k, PAD + t * cols : PAD + (t + 1) * cols, :] = value[:, 128 * k : 128 * k + 128]
+    tiles = [(1, t if plan.ring else lax.rem(col + (t - 5 + plan.n_col), plan.n_col)) for t in range(plan.tiles)]
+    tiles += [(0, lax.rem(col + (t - 1 + plan.n_col), plan.n_col)) for t in range(3)]
+    for at, (image, tile) in enumerate(tiles):
+        for dr in range(3):
+            source = jnp.clip(row + (dr - 1), 0, plan.n_row - 1) * plan.n_col + tile
+            v_ref[dr * rows : (dr + 1) * rows, at * cols : (at + 1) * cols] = g_ref[source, image]
+    value = lax.dot_general(v_ref[...], spread, TN, preferred_element_type=F32)
+    wide = plan.tiles * cols
     for k in range(4):
         ext_ref[k, 0:PAD, :] = jnp.zeros((PAD, 128), F32)
-        ext_ref[k, PAD + plan.tiles * cols :, :] = jnp.zeros((PAD, 128), F32)
-    for t in range(3):
-        tile = lax.rem(col + (t - 1 + plan.n_col), plan.n_col)
-        value = fetch(0, tile)
-        for k in range(4):
-            extl_ref[k, t * cols : (t + 1) * cols, :] = value[:, 128 * k : 128 * k + 128]
+        ext_ref[k, PAD : PAD + wide, :] = value[:wide, 128 * k : 128 * k + 128]
+        ext_ref[k, PAD + wide : 2 * PAD + wide, :] = jnp.zeros((PAD, 128), F32)
+        ext_ref[k, 2 * PAD + wide :, :] = value[wide:, 128 * k : 128 * k + 128]
 
     seg_id = iota((SEGS, 1), 0)
     if plan.ring:
@@ -151,145 +142,159 @@
         jnp.where((col == plan.n_col - 1) & (seg_id == SEGS - 1), 0.0, 1.0).astype(F32),
     )
     areas = (
-        (ext_ref, PAD, plan.seg, 0, edges_right),
-        (extl_ref, cols, plan.seg_left, plan.left_at, edges_left),
+        (PAD, plan.seg, 0, edges_right),
+        (2 * PAD + wide + cols, plan.seg_left, plan.left_at, edges_left),
     )
     px_lane = (iota((SEGS, 128), 1) // 16) % 4
-    for half in range(2):
-        for source, pad, seg, at, edges in areas:
-            for c in range(seg // 2 + 2):
-                groups = []
-                for k in range(2):
-                    value = None
-                    for px in range(4):
-                        x = 2 * c + px - 3
-                        piece = source[2 * half + k, pl.ds(pad + x, SEGS, stride=seg), :]
-                        if x < 0:
-                            piece = piece * edges[0]
-                        if x >= seg:
-                            piece = piece * edges[1]
-                        value = piece if value is None else jnp.where(px_lane == px, piece, value)
-                    groups.append(value)
-                f_ref[half, at + c * SEGS : at + (c + 1) * SEGS, :] = jnp.concatenate(
-                    groups, axis=1
-                ).astype(BF16)
+
+    def gather(pad, seg, at, edges, c):
+        known = isinstance(c, int)
+        for half in range(2):
+            groups = []
+            for k in range(2):
+                value = None
+                for px in range(4):
+                    x = 2 * c + px - 3
+                    piece = ext_ref[2 * half + k, pl.ds(pad + x, SEGS, stride=seg), :]
+                    if known and x < 0:
+                        piece = piece * edges[0]
+                    if known and x >= seg:
+                        piece = piece * edges[1]
+                    value = piece if value is None else jnp.where(px_lane == px, piece, value)
+                groups.append(value)
+            target = pl.ds(at + c * SEGS if known else pl.multiple_of(at + c * SEGS, SEGS), SEGS)
+            f_ref[half, target, :] = jnp.concatenate(groups, axis=1).astype(BF16)
+
+    for pad, seg, at, edges in areas:
+        quads = seg // 2
+        for c in (0, 1, quads, quads + 1):
+            gather(pad, seg, at, edges, c)
+
+        def inner(c, carry, pad=pad, seg=seg, at=at, edges=edges):
+            gather(pad, seg, at, edges, c)
+            return carry
+
+        lax.fori_loop(2, quads, inner, 0, unroll=6 if quads % 6 == 2 else 2)
 
     def clear_first(value):
         pieces = []
-        for _, _, seg, at, edges in areas:
+        for _, seg, at, edges in areas:
             end = at + (seg // 2 + 2) * SEGS
             pieces.append(value[at : at + SEGS] * edges[0])
             pieces.append(value[at + SEGS : end - SEGS])
             pieces.append(value[end - SEGS : end] * edges[1])
         return jnp.concatenate(pieces, axis=0)
 
+    pitch = plan.total
     for half in range(2):
-        def layer_one(step, carry):
+        for step in range(5):
             value = jnp.dot(f_ref[half], w1_ref[step], preferred_element_type=F32)
             value = jax.nn.relu(value + b_ref[0:1, :])
-            x1_ref[5 * half + step] = clear_first(value).astype(BF16)
-            return carry
-
-        lax.fori_loop(0, 5, layer_one, 0)
+            at = (5 * half + step) * pitch
+            x1_ref[at : at + pitch] = clear_first(value).astype(BF16)
 
     @pl.when(first_row)
     def _():
-        x1_ref[0] = jnp.zeros(x1_ref.shape[1:], BF16)
+        x1_ref[0:pitch] = jnp.zeros((pitch, plan.lanes), BF16)
 
     @pl.when(last_row)
     def _():
-        x1_ref[9] = jnp.zeros(x1_ref.shape[1:], BF16)
-
-    def four(source, weight, r, count):
-        value = jnp.dot(source[r, 0:count], weight[0], preferred_element_type=F32)
-        value += jnp.dot(source[r, SEGS : count + SEGS], weight[1], preferred_element_type=F32)
-        value += jnp.dot(source[r + 1, 0:count], weight[2], preferred_element_type=F32)
-        return value + jnp.dot(source[r + 1, SEGS : count + SEGS], weight[3], preferred_element_type=F32)
-
-    count_two = plan.total - SEGS
+        x1_ref[9 * pitch :] = jnp.zeros((pitch, plan.lanes), BF16)
+
+    def four(source, weight, start, count):
+        value = None
+        for k in range(4):
+            at = pl.multiple_of(start + (k // 2) * pitch + (k % 2) * SEGS, SEGS)
+            part = jnp.dot(source[pl.ds(at, count)], weight[k], preferred_element_type=F32)
+            value = part if value is None else value + part
+        return value
+
     odd = (iota((SEGS, plan.lanes), 1) // ch) % 2
 
-    def layer_two(r, carry):
-        value = jax.nn.relu(four(x1_ref, w2_ref, r, count_two) + b_ref[1:2, :])
-        x2_ref[r] = value.astype(BF16)
-        for _, _, seg, at, edges in areas:
-            end = at + (seg // 2 + 1) * SEGS
-            head = value[at : at + SEGS]
-            x2_ref[r, at : at + SEGS] = jnp.where(odd == 0, head * edges[0], head).astype(BF16)
-            tail = value[end - SEGS : end]
-            x2_ref[r, end - SEGS : end] = jnp.where(odd == 1, tail * edges[1], tail).astype(BF16)
+    def layer_two(i, carry):
+        start = i * (3 * pitch)
+        value = four(x1_ref, w2_ref, start, 3 * pitch - SEGS)
+        value = jax.nn.relu(value + b_ref[1:2, :])
+        x2_ref[pl.ds(pl.multiple_of(start, SEGS), 3 * pitch - SEGS)] = value.astype(BF16)
+        for k in range(3):
+            for _, seg, at, edges in areas:
+                for low in (True, False):
+                    base = k * pitch + at + (0 if low else (seg // 2) * SEGS)
+                    piece = value[base : base + SEGS]
+                    piece = jnp.where(odd == (0 if low else 1), piece * edges[0 if low else 1], piece)
+                    x2_ref[pl.ds(pl.multiple_of(start + base, SEGS), SEGS)] = piece.astype(BF16)
         return carry
 
-    lax.fori_loop(0, 9, layer_two, 0)
+    lax.fori_loop(0, 3, layer_two, 0)
 
     @pl.when(first_row)
     def _():
-        x2_ref[0, :, 0 : 2 * ch] = jnp.zeros((count_two, 2 * ch), BF16)
+        x2_ref[0:pitch, 0 : 2 * ch] = jnp.zeros((pitch, 2 * ch), BF16)
 
     @pl.when(last_row)
     def _():
-        x2_ref[8, :, 2 * ch :] = jnp.zeros((count_two, 2 * ch), BF16)
-
-    count_three = count_two - SEGS
+        x2_ref[8 * pitch :, 2 * ch :] = jnp.zeros((pitch, 2 * ch), BF16)
+
     per = plan.quads_left * SEGS
     group = iota((per, plan.lanes), 1) // ch
 
-    def layer_three(r, carry):
-        value = four(x2_ref, w3_ref, r, count_three) + b_ref[2:3, :]
-        x3_ref[r] = value[: plan.points].astype(BF16)
-        left = value[plan.left_at : plan.left_at + per]
-        swapped = jnp.concatenate(
-            [left[:, ch : 2 * ch], left[:, :ch], left[:, 3 * ch :], left[:, 2 * ch : 3 * ch]], axis=1
-        )
-        for dy in range(2):
-            for dxr in range(2):
-                for dxl in range(2):
-                    block = jnp.where(group == 2 * dy + dxr, left if dxl == dxr else swapped, 0.0)
-                    at = (4 * dy + 2 * dxr + dxl) * per
-                    lb_ref[r, at : at + per] = block.astype(BF16)
+    def layer_three(i, carry):
+        value = four(x2_ref, w3_ref, i * (2 * pitch), 2 * pitch - 2 * SEGS) + b_ref[2:3, :]
+        for k in range(2):
+            x3_ref[2 * i + k] = value[k * pitch : k * pitch + plan.points].astype(BF16)
+            left = value[k * pitch + plan.left_at : k * pitch + plan.left_at + per]
+            swapped = jnp.concatenate(
+                [left[:, ch : 2 * ch], left[:, :ch], left[:, 3 * ch :], left[:, 2 * ch : 3 * ch]], axis=1
+            )
+            for block in range(8):
+                dy, dxr, dxl = block // 4, (block // 2) % 2, block % 2
+                piece = jnp.where(group == 2 * dy + dxr, left if dxl == dxr else swapped, 0.0)
+                lb_ref[2 * i + k, block * per : (block + 1) * per] = piece.astype(BF16)
         return carry
 
-    lax.fori_loop(0, 8, layer_three, 0)
+    lax.fori_loop(0, 4, layer_three, 0)
 
     scale = math.log2(math.e) / math.sqrt(ch)
     pair = 2 * per
-
-    def score(r, carry):
-        s_ref[...] = lax.dot_general(x3_ref[r], lb_ref[r], NT, preferred_element_type=F32)
+    chunk = 32
+
+    def multiply(r, slot):
+        value = lax.dot_general(x3_ref[r], lb_ref[r], NT, preferred_element_type=F32)
+        tops = []
         for dy in range(2):
             lanes = slice(dy * 2 * pair, (dy + 1) * 2 * pair)
-
-            def find_top(i, top):
-                at = pl.ds(pl.multiple_of(i * 32, 32), 32)
-                value = s_ref[at, lanes] + bias_ref[at, :]
-                s_ref[at, lanes] = value
-                return jnp.maximum(top, jnp.max(value.reshape(4, 8, 2 * pair), axis=0))
-
-            top = lax.fori_loop(
-                0, plan.points // 32, find_top, jnp.full((8, 2 * pair), -1e30, F32), unroll=4
-            )
+            top = None
+            for at in range(0, plan.points, chunk):
+                piece = value[at : at + chunk, lanes] + bias_ref[at : at + chunk, :]
+                s_ref[slot, at : at + chunk, lanes] = piece
+                best = jnp.max(piece.reshape(chunk // 8, 8, 2 * pair), axis=0)
+                top = best if top is None else jnp.maximum(top, best)
             top = jnp.max(top, axis=0, keepdims=True)
             top = jnp.maximum(top[:, :pair], top[:, pair:])
-            top = jnp.broadcast_to(jnp.concatenate([top, top], axis=1), (8, 2 * pair))
-
-            def add_up(i, state):
-                total, moment = state
-                at = pl.ds(pl.multiple_of(i * 32, 32), 32)
-                value = s_ref[at, lanes].reshape(4, 8, 2 * pair) - top[None]
-                weight = jnp.exp2(value * scale)
+            tops.append(jnp.broadcast_to(jnp.concatenate([top, top], axis=1), (8, 2 * pair)))
+        return tuple(tops)
+
+    def weigh(r, slot, tops):
+        for dy in range(2):
+            lanes = slice(dy * 2 * pair, (dy + 1) * 2 * pair)
+            total = moment = jnp.zeros((8, 2 * pair), F32)
+            for at in range(0, plan.points, chunk):
+                value = s_ref[slot, at : at + chunk, lanes].reshape(chunk // 8, 8, 2 * pair)
+                weight = jnp.exp2((value - tops[dy][None]) * scale)
+                disp = disp_ref[at : at + chunk, :].reshape(chunk // 8, 8, 2 * pair)
                 total = total + jnp.sum(weight, axis=0)
-                moment = moment + jnp.sum(weight * disp_ref[at, :].reshape(4, 8, 2 * pair), axis=0)
-                return total, moment
-
-            zero = jnp.zeros((8, 2 * pair), F32)
-            total, moment = lax.fori_loop(0, plan.points // 32, add_up, (zero, zero), unroll=4)
+                moment = moment + jnp.sum(weight * disp, axis=0)
             total = jnp.sum(total, axis=0, keepdims=True)
             moment = jnp.sum(moment, axis=0, keepdims=True)
             tot_ref[pl.ds(2 * r + dy, 1), :] = total[:, :pair] + total[:, pair:]
             mom_ref[pl.ds(2 * r + dy, 1), :] = moment[:, :pair] + moment[:, pair:]
-        return carry
-
-    lax.fori_loop(0, 8, score, 0)
+
+    def score(r, tops):
+        later = multiply(r, r % 2)
+        weigh(r - 1, (r - 1) % 2, tops)
+        return later
+
+    weigh(7, 1, lax.fori_loop(1, 8, score, multiply(0, 0)))
 
     n, p = iota((pair, cols), 0), iota((pair, cols), 1)
     left = n % per
@@ -330,7 +335,7 @@
             ),
             in_specs=[vmem, vmem, vmem, smem, smem],
             out_specs=(vmem,) * 5,
-            compiler_params=pltpu.CompilerParams(vmem_limit_bytes=48 * 2**20),
+            compiler_params=pltpu.CompilerParams(vmem_limit_bytes=16 * 2**20),
         )(kernel_one, kernel_two, kernel_three, place, block_list.reshape(-1))
         biases = jnp.stack([jnp.tile(b, 4) for b in (bias_one, bias_two, bias_three)])
         return pl.pallas_call(
@@ -339,18 +344,18 @@
             in_specs=[smem] + [vmem] * 7,
             out_specs=vmem,
             scratch_shapes=[
-                pltpu.VMEM((4, plan.tiles * cols + 2 * PAD, 128), F32),
-                pltpu.VMEM((4, 3 * cols, 128), F32),
+                pltpu.VMEM((3 * rows, (plan.tiles + 3) * cols), BF16),
+                pltpu.VMEM((4, (plan.tiles + 3) * cols + 2 * PAD, 128), F32),
                 pltpu.VMEM((2, plan.total, 256), BF16),
-                pltpu.VMEM((10, plan.total, lanes), BF16),
-                pltpu.VMEM((9, plan.total - SEGS, lanes), BF16),
+                pltpu.VMEM((10 * plan.total, lanes), BF16),
+                pltpu.VMEM((9 * plan.total, lanes), BF16),
                 pltpu.VMEM((8, plan.points, lanes), BF16),
                 pltpu.VMEM((8, 2 * n_left, lanes), BF16),
-                pltpu.VMEM((plan.points, 2 * n_left), F32),
+                pltpu.VMEM((2, plan.points, 2 * n_left), F32),
                 pltpu.VMEM((rows, cols), F32),
                 pltpu.VMEM((rows, cols), F32),
             ],
-            compiler_params=pltpu.CompilerParams(vmem_limit_bytes=56 * 2**20),
+            compiler_params=pltpu.CompilerParams(vmem_limit_bytes=32 * 2**20),
         )(place, gathered, w1, biases, w2, w3, mask, disp)
 
     return jax.shard_map(

time: 43.7 us -> 36.5 us (0.84)
  Pallas kernels: 25.1 us -> 18.6 us
  local copies, waits for them, and re-layouts: 8.25 us -> 3.47 us
  waiting for transfers between devices: 0.65 us -> 5.28 us
  other arithmetic: 1.36 us -> 0.79 us
    pallas_call x1, Pallas kernels: 23.2 us -> 16.7 us  [per_device(): pl.pallas_call(functools.partial(main_kernel, plan), out_shape=jax.ShapeD...]
    unnamed x29 -> x15, local copies, waits for them, and re-layouts: 7.24 us -> 2.49 us
    all_to_all x1, waiting for transfers between devices: 0.65 us -> 5.28 us  [per_device(): lax.all_to_all(jnp.broadcast_to(images, (devices,) + images.shape), ('row...]
    another operation x1, other arithmetic: 0.58 us -> 0.01 us  [per_device(): jnp.stack([jnp.tile(b, 4) for b in (bias_one, bias_two, bias_three)])]
  transfers between devices with their start and end apart: 1 -> 1, of which waited for: 1 -> 1; matrix products, arithmetic and copies ran while one was open for 2% -> 1% of each run, Pallas kernels for 4% -> 5%
where the time goes in v1:
time: 36.5 us; the launch traced here: 36.1 us
  Pallas kernels  18.6 us (51%)
  starting transfers between devices  7.3 us (20%)
  waiting for transfers between devices  5.28 us (14%)
  local copies, waits for them, and re-layouts  3.47 us (10%)
  other arithmetic  0.79 us (2%)
  between operations  0.7 us (2%)
    pallas_call x1, Pallas kernels, per_device(): pl.pallas_call(functools.partial(main_kernel, plan), out_shape=jax.ShapeD...  16.7 us
    all_to_all x1, starting transfers between devices, per_device(): lax.all_to_all(jnp.broadcast_to(images, (devices,) + images.shape), ('row...  7.3 us
    all_to_all x1, waiting for transfers between devices, per_device(): lax.all_to_all(jnp.broadcast_to(images, (devices,) + images.shape), ('row...  5.28 us
    unnamed x15, local copies, waits for them, and re-layouts  2.49 us
    pallas_call x1, Pallas kernels, per_device(): pl.pallas_call(functools.partial(prep_kernel, plan), out_shape=(jax.Shape...  1.86 us
    broadcast_in_dim x1, local copies, waits for them, and re-layouts, per_device(): jnp.broadcast_to(images, (devices,) + images.shape)  0.73 us
  transfers between devices with their start and end apart: 1, of which 1 were waited for; matrix products, arithmetic and copies ran while one was open for 1% of the time, Pallas kernels for 5%

profile of v1, /device:TPU:0, one launch (start us, length us, event | category | flops | bytes accessed | tf_op | source)
XLA Modules:
  0.0 36.1 jit_solution(7635015299403298291)
XLA Ops:
  0.0 0.7 %pad_maximum_fusion = bf16[2,16,128]{2,1,0:T(8,128)(2,1)S(1)} fusion(bf16[1,16,128]{2,1,0:T(8,128)(2,1)} %bitcast.8, bf16[1,16,128]{2,1,0:T(8,128)(2,1)} %bitcast.9), kind=kLoop, calls=%fused_computation | loop fusion | flops 4096 | bytes 16384 | tf_op jit(solution)/shard_map/stack | solution.py:316
  0.7 0.7 %broadcast_in_dim.3 = bf16[32,2,16,128]{3,2,1,0:T(8,128)(2,1)} broadcast(bf16[2,16,128]{2,1,0:T(8,128)(2,1)S(1)} %pad_maximum_fusion), dimensions={1,2,3} | broadcast | bytes 270336 | tf_op jit(solution)/shard_map/broadcast_in_dim | solution.py:318
  1.4 0.0 copy-start
  1.4 0.0 copy-start.1
  1.4 7.3 %all-to-all-start = ((bf16[32,2,16,128]{3,2,1,0:T(8,128)(2,1)}), bf16[32,2,16,128]{3,2,1,0:T(8,128)(2,1)S(1)}, u32[]{:S(2)}, u32[]{:S(2)}) async-start(bf16[32,2,16,128]{3,2,1,0:T(8,128)(2,1)} %broadcast_in_dim.3), calls=%async_computation | async-start | bytes 524288 | tf_op jit(solution)/shard_map/all_to_all | solution.py:317
  8.8 0.0 copy-start.3
  9.4 0.0 copy-done.3
  9.5 0.0 copy-start.4
  9.5 0.1 copy.11.k1_ref
  9.5 0.6 %copy-done.4 = f32[64]{0:T(128)S(1)} copy-done((f32[64]{0:T(128)S(1)}, f32[64]{0:T(128)}, u32[]{:S(2)}) %copy-start.4) | copy-done | bytes 280
  10.1 0.0 copy-start.5
  10.1 0.1 stack_tile.11
  10.2 0.6 %copy-done.5 = f32[64]{0:T(128)S(1)} copy-done((f32[64]{0:T(128)S(1)}, f32[64]{0:T(128)}, u32[]{:S(2)}) %copy-start.5) | copy-done | bytes 280
  10.8 0.0 copy-start.6
  10.8 0.1 stack_tile.10
  10.9 0.6 %copy-done.6 = f32[64]{0:T(128)S(1)} copy-done((f32[64]{0:T(128)S(1)}, f32[64]{0:T(128)}, u32[]{:S(2)}) %copy-start.6) | copy-done | bytes 280
  11.4 0.1 stack_tile.9
  11.5 0.1 pad_add_fusion.place_ref
  11.6 0.0 copy-start.2
  11.6 0.0 copy-done
  11.6 0.0 copy-done.1
  11.6 0.6 %copy-done.2 = s32[1,1,8]{2,1,0:T(1,128)S(1)} copy-done((s32[1,1,8]{2,1,0:T(1,128)S(1)}, s32[1,1,8]{2,1,0:T(1,128)}, u32[]{:S(2)}) %copy-start.2) | copy-done | bytes 56
  12.2 1.9 %shard_map.100 = (bf16[5,256,256]{2,1,0:T(8,128)(2,1)S(1)}, bf16[4,256,256]{2,1,0:T(8,128)(2,1)S(1)}, bf16[4,256,256]{2,1,0:T(8,128)(2,1)S(1)}, f32[512,256]{1,0:T(8,128)S(1)}, f32[512,256]{1,0:T(8,128)S(1)}) custom-call(f32[64,9]{1,0:T(8,128)S(1)} %copy.11.k1_ref, bf16[9,64,64]{2,1,0:T(8,128)(2,1)S(1)} %copy-done, bf16[9,64,64]{2,1,0:T(8,128)(2,1)S(1)} %copy-done.1, ...), custom_call_target="tpu_custom_call" | custom-call | tf_op jit(solution)/shard_map/pallas_call | solution.py:327
  14.1 5.3 %all-to-all-done.g_ref = bf16[32,2,16,128]{3,2,1,0:T(8,128)(2,1)S(1)} async-done(((bf16[32,2,16,128]{3,2,1,0:T(8,128)(2,1)}), bf16[32,2,16,128]{3,2,1,0:T(8,128)(2,1)S(1)}, u32[]{:S(2)}, u32[]{:S(2)}) %all-to-all-start) | async-done | bytes 262176 | tf_op jit(solution)/shard_map/all_to_all | solution.py:317
  19.4 16.7 %shard_map.101 = f32[16,128]{1,0:T(8,128)} custom-call(s32[3]{0:T(128)S(1)} %pad_add_fusion.place_ref, bf16[32,2,16,128]{3,2,1,0:T(8,128)(2,1)S(1)} %all-to-all-done.g_ref, bf16[5,256,256]{2,1,0:T(8,128)(2,1)S(1)} %get-tuple-element.10.w1_ref, f32[3,256]{1,0:T(4,128)S(1)} %pad_maximum_fusion.1.b_ref, bf16[4,256,256]{2,1,0:T(8,128)(2,1)S(1)} %get-tuple-element.11.w2_ref, ...), custom_call_target="tpu_custom_call" | custom-call | tf_op jit(solution)/shard_map/pallas_call | solution.py:341
  (4 shorter events, 0.0 us)
Async XLA Ops:
  1.4 10.1 %copy-start = (bf16[9,64,64]{2,1,0:T(8,128)(2,1)S(1)}, bf16[9,64,64]{2,1,0:T(8,128)(2,1)}, u32[]{:S(2)}) copy-start(bf16[9,64,64]{2,1,0:T(8,128)(2,1)} %k2_ref.1) | copy-start | bytes 221188
  1.4 10.1 %copy-start.1 = (bf16[9,64,64]{2,1,0:T(8,128)(2,1)S(1)}, bf16[9,64,64]{2,1,0:T(8,128)(2,1)}, u32[]{:S(2)}) copy-start(bf16[9,64,64]{2,1,0:T(8,128)(2,1)} %k3_ref.1) | copy-start | bytes 221188
  1.4 18.0 %all-to-all-start = ((bf16[32,2,16,128]{3,2,1,0:T(8,128)(2,1)}), bf16[32,2,16,128]{3,2,1,0:T(8,128)(2,1)S(1)}, u32[]{:S(2)}, u32[]{:S(2)}) async-start(bf16[32,2,16,128]{3,2,1,0:T(8,128)(2,1)} %broadcast_in_dim.3), calls=%async_computation | async-start | bytes 524288 | tf_op jit(solution)/shard_map/all_to_all | solution.py:317
  8.8 0.7 %copy-start.3 = (f32[64,9]{0,1:T(8,128)S(1)}, f32[64,9]{0,1:T(8,128)}, u32[]{:S(2)}) copy-start(f32[64,9]{0,1:T(8,128)} %param.12) | copy-start | bytes 6916
  9.5 0.7 %copy-start.4 = (f32[64]{0:T(128)S(1)}, f32[64]{0:T(128)}, u32[]{:S(2)}) copy-start(f32[64]{0:T(128)} %param.17) | copy-start | bytes 772
  10.1 0.7 %copy-start.5 = (f32[64]{0:T(128)S(1)}, f32[64]{0:T(128)}, u32[]{:S(2)}) copy-start(f32[64]{0:T(128)} %param.15) | copy-start | bytes 772
  10.8 0.7 %copy-start.6 = (f32[64]{0:T(128)S(1)}, f32[64]{0:T(128)}, u32[]{:S(2)}) copy-start(f32[64]{0:T(128)} %param.13) | copy-start | bytes 772
  11.6 0.7 %copy-start.2 = (s32[1,1,8]{2,1,0:T(1,128)S(1)}, s32[1,1,8]{2,1,0:T(1,128)}, u32[]{:S(2)}) copy-start(s32[1,1,8]{2,1,0:T(1,128)} %param.18) | copy-start | bytes 100

commit v2 on v1

v2 whole, which is shorter than its diff:
```python
import functools
import math

import jax
import jax.numpy as jnp
from jax import lax
from jax.experimental import pallas as pl
from jax.experimental.pallas import tpu as pltpu
from jax.sharding import PartitionSpec as P

DBLOCK = 64
SPAN = 4
SEGS = 16
NT = (((1,), (1,)), ((), ()))
F32 = jnp.float32
BF16 = jnp.bfloat16


def iota(shape, dim):
    return lax.broadcasted_iota(jnp.int32, shape, dim)


class Plan:
    def __init__(self, mesh, rows, cols, chans):
        self.n_row, self.n_col = mesh.shape["row"], mesh.shape["col"]
        self.rows, self.cols, self.chans = rows, cols, chans
        self.ring = self.n_col == 2 * SPAN
        self.tiles = self.n_col if self.ring else 16
        self.width = self.n_col * cols
        self.seg = self.tiles * cols // SEGS
        self.quads = self.seg // 2
        self.seg_left = cols // SEGS
        self.quads_left = self.seg_left // 2
        self.left_at = (self.quads + 2) * SEGS
        self.total = self.left_at + (self.quads_left + 2) * SEGS
        self.points = self.quads * SEGS
        self.lanes = 4 * chans


def prep_kernel(
    plan, k1_ref, b1_ref, k2_ref, b2_ref, k3_ref, b3_ref, place_ref, list_ref,
    w1_ref, w2_ref, w3_ref, b_ref, mask_ref, disp_ref, spread_ref,
):
    ch = plan.chans
    kernel = k1_ref[...]
    high = kernel.astype(BF16)
    rest = kernel - high.astype(F32)
    middle = rest.astype(BF16)
    low = (rest - middle.astype(F32)).astype(BF16)
    taps = kernel.shape[0]
    w1_ref[...] = jnp.zeros(w1_ref.shape, BF16)
    for part, values in enumerate((high, middle, low)):
        for out in range(4):
            oy, ox = divmod(out, 2)
            row, tap = iota((5 * 64, taps), 0), iota((5 * 64, taps), 1)
            step, px, y = row // 64, (row // 16) % 4, row % 16
            pick = (px == tap % 3 + ox) & (y == 2 * step + oy + tap // 3)
            pick = jnp.where(pick, 1.0, 0.0).astype(BF16)
            block = jnp.dot(pick, values, preferred_element_type=F32).astype(BF16)
            for step in range(5):
                w1_ref[step, part * 64 : part * 64 + 64, out * ch : out * ch + ch] = block[
                    step * 64 : step * 64 + 64
                ]
    for layer, bias in enumerate((b1_ref, b2_ref, b3_ref)):
        b_ref[layer : layer + 1, :] = jnp.concatenate([bias[...]] * 4, axis=1)
    for source, target in ((k2_ref, w2_ref), (k3_ref, w3_ref)):
        turned = [source[tap].astype(F32).T for tap in range(9)]
        nothing = jnp.zeros((ch, ch), F32)
        for py in range(4):
            for px in range(4):
                pieces = []
                for out in range(4):
                    ty, tx = py - out // 2, px - out % 2
                    inside = 0 <= ty < 3 and 0 <= tx < 3
                    pieces.append(turned[3 * ty + tx] if inside else nothing)
                quad, sub = (py // 2) * 2 + px // 2, (py % 2) * 2 + px % 2
                at = (4 * quad + sub) * ch
                target[at : at + ch, :] = jnp.concatenate(pieces, axis=1).astype(BF16)
    col = place_ref[1]
    bits = jnp.int32(0)
    for k in range(list_ref.shape[0]):
        bits = bits | jnp.where(k < place_ref[2], jnp.left_shift(jnp.int32(1), list_ref[k]), 0)
    reach = SPAN * plan.cols
    shape = (plan.points, 4 * SEGS * plan.quads_left)
    m, n = iota(shape, 0), iota(shape, 1)
    per = SEGS * plan.quads_left
    q = (m % SEGS) * plan.seg + 2 * (m // SEGS) + n // (2 * per)
    left = n % per
    p = (left % SEGS) * plan.seg_left + 2 * (left // SEGS) + (n // per) % 2
    if plan.ring:
        d = col * plan.cols + p - q
        d = jnp.where(d < -reach, d + plan.width, d)
        d = jnp.where(d >= reach, d - plan.width, d)
        listed = jnp.right_shift(bits, (d + reach) // DBLOCK) & 1
    else:
        d = 5 * plan.cols + p - q
        inside = (d >= -reach) & (d < reach)
        block = jnp.where(inside, (d + reach) // DBLOCK, 31)
        listed = jnp.where(inside, jnp.right_shift(bits, block) & 1, 0)
    mask_ref[...] = jnp.where(listed > 0, 0.0, -1e30).astype(F32)
    disp_ref[...] = d.astype(F32)

    row = place_ref[0]
    k, n = iota((256, 1), 0), iota((1, 512), 1)
    y = 10 * (n // 256) + n % 16
    wanted = jnp.where((y < plan.rows + 6) & (n % 256 < 192), (n // 16) % 4 * 64 + plan.rows - 3 + y, -1)
    v = k % 64
    hidden = ((row == 0) & (v < plan.rows)) | ((row == plan.n_row - 1) & (v >= 2 * plan.rows))
    spread_ref[...] = jnp.where(wanted == jnp.where(hidden, -2, k), 1.0, 0.0).astype(BF16)


def main_kernel(
    plan, place_ref, g_ref, spread_ref, w1_ref, b_ref, w2_ref, w3_ref, mask_at, disp_at, out_ref,
    v_ref, v4_ref, fx_ref, f_ref, x1_ref, x2_ref, x3_ref, lb_ref, s_ref, tot_ref, mom_ref,
    mask_ref, disp_ref, sems,
):
    rows, cols, ch = plan.rows, plan.cols, plan.chans
    row, col = place_ref[0], place_ref[1]
    first_row, last_row = row == 0, row == plan.n_row - 1
    copies = [
        pltpu.make_async_copy(source, target, sems.at[k])
        for k, (source, target) in enumerate(((mask_at, mask_ref), (disp_at, disp_ref)))
    ]
    for copy in copies:
        copy.start()

    tiles = [(1, t if plan.ring else lax.rem(col + (t - 5 + plan.n_col), plan.n_col)) for t in range(plan.tiles)]
    tiles += [(0, lax.rem(col + (t - 1 + plan.n_col), plan.n_col)) for t in range(3)]
    for at, (image, tile) in enumerate(tiles):
        for dr in range(3):
            source = jnp.clip(row + (dr - 1), 0, plan.n_row - 1) * plan.n_col + tile
            v_ref[dr * rows : (dr + 1) * rows, at * cols : (at + 1) * cols] = g_ref[source, image].astype(F32)
    for px in range(4):
        moved = v_ref[...] if px == 1 else pltpu.roll(v_ref[...], (1 - px) % v_ref.shape[1], 1)
        v4_ref[px * 64 : px * 64 + 3 * rows, :] = moved.astype(BF16)
        v4_ref[px * 64 + 3 * rows : px * 64 + 64, :] = jnp.zeros((64 - 3 * rows, v_ref.shape[1]), BF16)
    wide = plan.tiles * cols
    seg_id = iota((SEGS, 1), 0)
    if plan.ring:
        begin = seg_id * plan.seg
    else:
        begin = lax.rem((col + plan.n_col - 5) * cols + seg_id * plan.seg, plan.width)
    edges_right = (
        jnp.where(begin == 0, 0.0, 1.0).astype(F32),
        jnp.where(begin + plan.seg == plan.width, 0.0, 1.0).astype(F32),
    )
    edges_left = (
        jnp.where((col == 0) & (seg_id == 0), 0.0, 1.0).astype(F32),
        jnp.where((col == plan.n_col - 1) & (seg_id == SEGS - 1), 0.0, 1.0).astype(F32),
    )
    areas = (
        (plan.seg, 0, edges_right),
        (plan.seg_left, plan.left_at, edges_left),
    )
    px_lane = iota((SEGS, 256), 1) // 64
    for start, before, size, (seg, at, edges) in ((0, 0, wide, areas[0]), (wide, cols, 3 * cols, areas[1])):
        count = (seg // 2 + 2) * SEGS
        n, k = iota((count, 1), 0), iota((1, size), 1)
        pick = jnp.where(before + (n % SEGS) * seg + 2 * (n // SEGS) - 2 == k, 1.0, 0.0).astype(BF16)
        value = lax.dot_general(pick, v4_ref[:, start : start + size], NT, preferred_element_type=F32)
        fx_ref[at : at + count, :] = value.astype(BF16)
        low = value[SEGS : 2 * SEGS]
        fx_ref[at + SEGS : at + 2 * SEGS, :] = jnp.where(px_lane == 0, low * edges[0], low).astype(BF16)
        high = value[count - 2 * SEGS : count - SEGS]
        fx_ref[at + count - 2 * SEGS : at + count - SEGS, :] = jnp.where(
            px_lane == 3, high * edges[1], high
        ).astype(BF16)
    for half in range(2):
        value = jnp.dot(
            fx_ref[...], spread_ref[:, half * 256 : half * 256 + 256], preferred_element_type=F32
        )
        f_ref[half] = value.astype(BF16)

    def clear_first(value):
        pieces = []
        for seg, at, edges in areas:
            end = at + (seg // 2 + 2) * SEGS
            pieces.append(value[at : at + SEGS] * edges[0])
            pieces.append(value[at + SEGS : end - SEGS])
            pieces.append(value[end - SEGS : end] * edges[1])
        return jnp.concatenate(pieces, axis=0)

    pitch = plan.total

    def layer_one(half, carry):
        for step in range(5):
            value = jnp.dot(f_ref[half], w1_ref[step], preferred_element_type=F32)
            value = clear_first(jax.nn.relu(value + b_ref[0:1, :]))
            x1_ref[pl.ds(pl.multiple_of((5 * half + step) * pitch, SEGS), pitch)] = value.astype(BF16)
        return carry

    lax.fori_loop(0, 2, layer_one, 0)

    @pl.when(first_row)
    def _():
        x1_ref[0:pitch] = jnp.zeros((pitch, plan.lanes), BF16)

    @pl.when(last_row)
    def _():
        x1_ref[9 * pitch :] = jnp.zeros((pitch, plan.lanes), BF16)

    def four(source, weight, start, count):
        value = None
        for k in range(4):
            at = pl.multiple_of(start + (k // 2) * pitch + (k % 2) * SEGS, SEGS)
            part = jnp.dot(source[pl.ds(at, count)], weight[k * 256 : k * 256 + 256], preferred_element_type=F32)
            value = part if value is None else value + part
        return value

    odd = (iota((SEGS, plan.lanes), 1) // ch) % 2

    def layer_two(i, carry):
        start = i * (3 * pitch)
        value = four(x1_ref, w2_ref, start, 3 * pitch - SEGS)
        value = jax.nn.relu(value + b_ref[1:2, :])
        x2_ref[pl.ds(pl.multiple_of(start, SEGS), 3 * pitch - SEGS)] = value.astype(BF16)
        for k in range(3):
            for seg, at, edges in areas:
                for low in (True, False):
                    base = k * pitch + at + (0 if low else (seg // 2) * SEGS)
                    piece = value[base : base + SEGS]
                    piece = jnp.where(odd == (0 if low else 1), piece * edges[0 if low else 1], piece)
                    x2_ref[pl.ds(pl.multiple_of(start + base, SEGS), SEGS)] = piece.astype(BF16)
        return carry

    lax.fori_loop(0, 3, layer_two, 0)

    @pl.when(first_row)
    def _():
        x2_ref[0:pitch, 0 : 2 * ch] = jnp.zeros((pitch, 2 * ch), BF16)

    @pl.when(last_row)
    def _():
        x2_ref[8 * pitch : 9 * pitch, 2 * ch :] = jnp.zeros((pitch, 2 * ch), BF16)

    per = plan.quads_left * SEGS
    group = iota((per, plan.lanes), 1) // ch

    chunk = 256
    chunks = plan.points // chunk

    def patch(r, at, count):
        base = r * pitch + at
        return jnp.concatenate(
            [
                x2_ref[pl.ds(pl.multiple_of(base + (k // 2) * pitch + (k % 2) * SEGS, SEGS), count)]
                for k in range(4)
            ],
            axis=1,
        )

    def layer_three(r, slot, u):
        value = jnp.dot(patch(r, u * chunk, chunk), w3_ref[...], preferred_element_type=F32)
        x3_ref[slot, u * chunk : (u + 1) * chunk] = (value + b_ref[2:3, :]).astype(BF16)

    def layer_three_left(r, slot):
        left = jnp.dot(patch(r, plan.left_at, per), w3_ref[...], preferred_element_type=F32) + b_ref[2:3, :]
        swapped = jnp.concatenate(
            [left[:, ch : 2 * ch], left[:, :ch], left[:, 3 * ch :], left[:, 2 * ch : 3 * ch]], axis=1
        )
        for block in range(8):
            dy, dxr, dxl = block // 4, (block // 2) % 2, block % 2
            piece = jnp.where(group == 2 * dy + dxr, left if dxl == dxr else swapped, 0.0)
            lb_ref[slot, block * per : (block + 1) * per] = piece.astype(BF16)

    scale = math.log2(math.e) / math.sqrt(ch)
    pair = 2 * per
    step = 32

    def multiply(slot, u, top):
        value = lax.dot_general(
            x3_ref[slot, u * chunk : (u + 1) * chunk], lb_ref[slot], NT, preferred_element_type=F32
        )
        for at in range(0, chunk, step):
            row_at = slice(u * chunk + at, u * chunk + at + step)
            mask = mask_ref[row_at, :]
            piece = value[at : at + step] + jnp.concatenate([mask, mask], axis=1)
            s_ref[slot, row_at, :] = piece
            best = jnp.max(piece.reshape(step // 8, 8, 4 * pair), axis=0)
            top = best if top is None else jnp.maximum(top, best)
        return top

    def spread_top(top):
        top = jnp.max(top, axis=0, keepdims=True)
        parts = []
        for dy in range(2):
            low, high = top[:, 2 * dy * pair : (2 * dy + 1) * pair], top[:, (2 * dy + 1) * pair : (2 * dy + 2) * pair]
            parts += [jnp.maximum(low, high)] * 2
        return jnp.broadcast_to(jnp.concatenate(parts, axis=1), (8, 4 * pair))

    def weigh(slot, u, top, state):
        state = list(state)
        for at in range(0, chunk, step):
            row_at = slice(u * chunk + at, u * chunk + at + step)
            disp = disp_ref[row_at, :].reshape(step // 8, 8, 2 * pair)
            for dy in range(2):
                lanes = slice(dy * 2 * pair, (dy + 1) * 2 * pair)
                value = s_ref[slot, row_at, lanes].reshape(step // 8, 8, 2 * pair)
                weight = jnp.exp2((value - top[:, lanes][None]) * scale)
                state[2 * dy] = state[2 * dy] + jnp.sum(weight, axis=0)
                state[2 * dy + 1] = state[2 * dy + 1] + jnp.sum(weight * disp, axis=0)
        return state

    def keep_sums(r, state):
        for dy in range(2):
            for target, value in ((tot_ref, state[2 * dy]), (mom_ref, state[2 * dy + 1])):
                value = jnp.sum(value, axis=0, keepdims=True)
                target[pl.ds(2 * r + 2 + dy, 1), :] = value[:, :pair] + value[:, pair:]

    none = [jnp.zeros((8, 2 * pair), F32)] * 4
    layer_three_left(0, 0)
    for u in range(chunks):
        layer_three(0, 0, u)
    for copy in copies:
        copy.wait()

    def together(j, top):
        for k in range(2):
            state, later = none, None
            layer_three_left(2 * j + k + 1, 1 - k)
            for u in range(chunks):
                layer_three(2 * j + k + 1, 1 - k, u)
                state = weigh(1 - k, u, top, state)
                later = multiply(k, u, later)
            keep_sums(2 * j + k - 1, state)
            top = spread_top(later)
        return top

    top = lax.fori_loop(0, 4, together, jnp.zeros((8, 4 * pair), F32))
    state = none
    for u in range(chunks):
        state = weigh(1, u, top, state)
    keep_sums(7, state)

    n, p = iota((pair, cols), 0), iota((pair, cols), 1)
    left = n % per
    place = (left % SEGS) * plan.seg_left + 2 * (left // SEGS) + n // per
    turn = jnp.where(place == p, 1.0, 0.0).astype(F32)
    value = mom_ref[2 : rows + 2, :] / tot_ref[2 : rows + 2, :] * (1.0 / cols)
    out_ref[...] = jnp.dot(value, turn, precision=lax.Precision.HIGHEST, preferred_element_type=F32)


def solution(mesh):
    def per_device(
        left_image, right_image, kernel_one, bias_one, kernel_two, bias_two,
        kernel_three, bias_three, block_list, block_count,
    ):
        rows, cols = left_image.shape
        ch = kernel_one.shape[0]
        plan = Plan(mesh, rows, cols, ch)
        devices = plan.n_row * plan.n_col
        images = jnp.stack([left_image, right_image])
        gathered = lax.all_to_all(
            jnp.broadcast_to(images, (devices,) + images.shape), ("row", "col"), 0, 0
        )
        place = jnp.stack(
            [lax.axis_index("row"), lax.axis_index("col"), block_count[0, 0]]
        ).astype(jnp.int32)
        vmem = pl.BlockSpec(memory_space=pltpu.VMEM)
        smem = pl.BlockSpec(memory_space=pltpu.SMEM)
        lanes = plan.lanes
        n_left = 4 * SEGS * plan.quads_left
        w1, w2, w3, biases, mask, disp, spread = pl.pallas_call(
            functools.partial(prep_kernel, plan),
            out_shape=(
                jax.ShapeDtypeStruct((5, 256, lanes), BF16),
                jax.ShapeDtypeStruct((4 * lanes, lanes), BF16),
                jax.ShapeDtypeStruct((4 * lanes, lanes), BF16),
                jax.ShapeDtypeStruct((3, lanes), F32),
                jax.ShapeDtypeStruct((plan.points, n_left), F32),
                jax.ShapeDtypeStruct((plan.points, n_left), F32),
                jax.ShapeDtypeStruct((256, 512), BF16),
            ),
            in_specs=[vmem] * 6 + [smem, smem],
            out_specs=(vmem,) * 7,
            compiler_params=pltpu.CompilerParams(vmem_limit_bytes=(12 if plan.ring else 24) * 2**20),
        )(
            kernel_one.T, bias_one[None], kernel_two, bias_two[None], kernel_three, bias_three[None],
            place, block_list.reshape(-1),
        )
        return pl.pallas_call(
            functools.partial(main_kernel, plan),
            out_shape=jax.ShapeDtypeStruct((rows, cols), F32),
            in_specs=[smem] + [vmem] * 6 + [pl.BlockSpec(memory_space=pltpu.HBM)] * 2,
            out_specs=vmem,
            scratch_shapes=[
                pltpu.VMEM((3 * rows, (plan.tiles + 3) * cols), F32),
                pltpu.VMEM((256, (plan.tiles + 3) * cols), BF16),
                pltpu.VMEM((plan.total, 256), BF16),
                pltpu.VMEM((2, plan.total, 256), BF16),
                pltpu.VMEM((10 * plan.total, lanes), BF16),
                pltpu.VMEM((10 * plan.total, lanes), BF16),
                pltpu.VMEM((2, plan.points, lanes), BF16),
                pltpu.VMEM((2, 2 * n_left, lanes), BF16),
                pltpu.VMEM((2, plan.points, 2 * n_left), F32),
                pltpu.VMEM((rows + 4, cols), F32),
                pltpu.VMEM((rows + 4, cols), F32),
                pltpu.VMEM((plan.points, n_left), F32),
                pltpu.VMEM((plan.points, n_left), F32),
                pltpu.SemaphoreType.DMA((2,)),
            ],
            compiler_params=pltpu.CompilerParams(vmem_limit_bytes=(18 if plan.ring else 44) * 2**20),
        )(place, gathered, spread, w1, biases, w2, w3, mask, disp)

    return jax.shard_map(
        per_device,
        mesh=mesh,
        in_specs=(
            P("row", "col"), P("row", "col"), P(), P(), P(), P(), P(), P(),
            P("row", "col", None), P("row", "col"),
        ),
        out_specs=P("row", "col"),
        check_vma=False,
    )
```

time: 36.5 us -> 33.5 us (0.918)
  Pallas kernels: 18.6 us -> 15.7 us
  local copies, waits for them, and re-layouts: 3.47 us -> 2.33 us
  waiting for transfers between devices: 5.28 us -> 6.37 us
    pallas_call x1, Pallas kernels: 16.7 us -> 13.7 us  [per_device(): pl.pallas_call(functools.partial(main_kernel, plan), out_shape=jax.ShapeD...]
    all_to_all x1, waiting for transfers between devices: 5.28 us -> 6.37 us  [per_device(): lax.all_to_all(jnp.broadcast_to(images, (devices,) + images.shape), ('row...]
    unnamed x15 -> x14, local copies, waits for them, and re-layouts: 2.49 us -> 1.6 us
  transfers between devices with their start and end apart: 1 -> 1, of which waited for: 1 -> 1; matrix products, arithmetic and copies ran while one was open for 1% -> 0% of each run, Pallas kernels for 5% -> 6%
where the time goes in v2:
time: 33.5 us; the launch traced here: 33.1 us
  Pallas kernels  15.7 us (47%)
  starting transfers between devices  7.3 us (22%)
  waiting for transfers between devices  6.37 us (19%)
  local copies, waits for them, and re-layouts  2.33 us (7%)
  other arithmetic  0.78 us (2%)
  between operations  0.7 us (2%)
    pallas_call x1, Pallas kernels, per_device(): pl.pallas_call(functools.partial(main_kernel, plan), out_shape=jax.ShapeD...  13.7 us
    all_to_all x1, starting transfers between devices, per_device(): lax.all_to_all(jnp.broadcast_to(images, (devices,) + images.shape), ('row...  7.3 us
    all_to_all x1, waiting for transfers between devices, per_device(): lax.all_to_all(jnp.broadcast_to(images, (devices,) + images.shape), ('row...  6.37 us
    pallas_call x1, Pallas kernels, per_device(): pl.pallas_call(functools.partial(prep_kernel, plan), out_shape=(jax.Shape...  1.92 us
    unnamed x14, local copies, waits for them, and re-layouts  1.6 us
    broadcast_in_dim x1, local copies, waits for them, and re-layouts, per_device(): jnp.broadcast_to(images, (devices,) + images.shape)  0.73 us
    another operation x1, other arithmetic, per_device(): images = jnp.stack([left_image, right_image])  0.71 us
  transfers between devices with their start and end apart: 1, of which 1 were waited for; matrix products, arithmetic and copies ran while one was open for 0% of the time, Pallas kernels for 6%

profile of v2, /device:TPU:0, one launch (start us, length us, event | category | flops | bytes accessed | tf_op | source)
XLA Modules:
  0.0 33.1 jit_solution(14831685901988459586)
XLA Ops:
  0.0 0.7 %pad_maximum_fusion = bf16[2,16,128]{2,1,0:T(8,128)(2,1)S(1)} fusion(bf16[1,16,128]{2,1,0:T(8,128)(2,1)} %bitcast.16, bf16[1,16,128]{2,1,0:T(8,128)(2,1)} %bitcast.17), kind=kLoop, calls=%fused_computation | loop fusion | flops 4096 | bytes 16384 | tf_op jit(solution)/shard_map/stack | solution.py:352
  0.7 0.7 %broadcast_in_dim.12 = bf16[32,2,16,128]{3,2,1,0:T(8,128)(2,1)} broadcast(bf16[2,16,128]{2,1,0:T(8,128)(2,1)S(1)} %pad_maximum_fusion), dimensions={1,2,3} | broadcast | bytes 270336 | tf_op jit(solution)/shard_map/broadcast_in_dim | solution.py:354
  1.4 0.0 copy-start
  1.4 7.3 %all-to-all-start = ((bf16[32,2,16,128]{3,2,1,0:T(8,128)(2,1)}), bf16[32,2,16,128]{3,2,1,0:T(8,128)(2,1)S(1)}, u32[]{:S(2)}, u32[]{:S(2)}) async-start(bf16[32,2,16,128]{3,2,1,0:T(8,128)(2,1)} %broadcast_in_dim.12), calls=%async_computation | async-start | bytes 524288 | tf_op jit(solution)/shard_map/all_to_all | solution.py:353
  9.4 0.0 copy-start.2
  9.4 0.0 copy-start.6
  9.4 0.1 pad_add_fusion.place_ref
  9.5 0.0 copy-start.3
  9.5 0.0 copy-start.4
  9.5 0.0 copy-start.5
  9.5 0.0 copy-done
  9.5 0.6 %copy-done.2 = f32[64,9]{0,1:T(8,128)S(1)} copy-done((f32[64,9]{0,1:T(8,128)S(1)}, f32[64,9]{0,1:T(8,128)}, u32[]{:S(2)}) %copy-start.2) | copy-done | bytes 2328
  10.1 0.0 copy-done.6
  10.1 0.1 copy-done.3
  10.2 0.0 copy-done.4
  10.2 0.0 copy-done.5
  10.2 0.0 copy-start.1
  10.2 0.9 %copy-done.1 = bf16[9,64,64]{2,1,0:T(8,128)(2,1)S(1)} copy-done((bf16[9,64,64]{2,1,0:T(8,128)(2,1)S(1)}, bf16[9,64,64]{2,1,0:T(8,128)(2,1)}, u32[]{:S(2)}) %copy-start.1) | copy-done | bytes 73752
  11.1 1.9 %shard_map.100 = (bf16[5,256,256]{2,1,0:T(8,128)(2,1)S(1)}, bf16[1024,256]{1,0:T(8,128)(2,1)S(1)}, bf16[1024,256]{1,0:T(8,128)(2,1)S(1)}, f32[3,256]{1,0:T(4,128...) custom-call(f32[9,64]{1,0:T(8,128)S(1)} %bitcast.11, f32[1,64]{1,0:T(1,128)S(1)} %bitcast.12, ...), custom_call_target="tpu_custom_call" | custom-call | tf_op jit(solution)/shard_map/pallas_call | solution.py:363
  13.0 6.4 %all-to-all-done.g_ref = bf16[32,2,16,128]{3,2,1,0:T(8,128)(2,1)S(1)} async-done(((bf16[32,2,16,128]{3,2,1,0:T(8,128)(2,1)}), bf16[32,2,16,128]{3,2,1,0:T(8,128)(2,1)S(1)}, u32[]{:S(2)}, u32[]{:S(2)}) %all-to-all-start) | async-done | bytes 262176 | tf_op jit(solution)/shard_map/all_to_all | solution.py:353
  19.4 13.7 %shard_map.101 = f32[16,128]{1,0:T(8,128)} custom-call(s32[3]{0:T(128)S(1)} %pad_add_fusion.place_ref, bf16[32,2,16,128]{3,2,1,0:T(8,128)(2,1)S(1)} %all-to-all-done.g_ref, bf16[256,512]{1,0:T(8,128)(2,1)S(1)} %get-tuple-element.12.spread_ref, bf16[5,256,256]{2,1,0:T(8,128)(2,1)S(1)} %get-tuple-element.13.w1_ref, f32[3,256]{1,0:T(4,128)S(1)} %get-tuple-element.14.b_ref, ...), custom_call_target="tpu_custom_call" | custom-call | tf_op jit(solution)/shard_map/pallas_call | solution.py:381
Async XLA Ops:
  1.4 8.1 %copy-start = (bf16[9,64,64]{2,1,0:T(8,128)(2,1)S(1)}, bf16[9,64,64]{2,1,0:T(8,128)(2,1)}, u32[]{:S(2)}) copy-start(bf16[9,64,64]{2,1,0:T(8,128)(2,1)} %k2_ref.1) | copy-start | bytes 221188
  1.4 18.0 %all-to-all-start = ((bf16[32,2,16,128]{3,2,1,0:T(8,128)(2,1)}), bf16[32,2,16,128]{3,2,1,0:T(8,128)(2,1)S(1)}, u32[]{:S(2)}, u32[]{:S(2)}) async-start(bf16[32,2,16,128]{3,2,1,0:T(8,128)(2,1)} %broadcast_in_dim.12), calls=%async_computation | async-start | bytes 524288 | tf_op jit(solution)/shard_map/all_to_all | solution.py:353
  9.4 0.7 %copy-start.2 = (f32[64,9]{0,1:T(8,128)S(1)}, f32[64,9]{0,1:T(8,128)}, u32[]{:S(2)}) copy-start(f32[64,9]{0,1:T(8,128)} %param.12) | copy-start | bytes 6916
  9.4 0.7 %copy-start.6 = (s32[1,1,8]{2,1,0:T(1,128)S(1)}, s32[1,1,8]{2,1,0:T(1,128)}, u32[]{:S(2)}) copy-start(s32[1,1,8]{2,1,0:T(1,128)} %param.18) | copy-start | bytes 100
  9.5 0.7 %copy-start.3 = (f32[64]{0:T(128)S(1)}, f32[64]{0:T(128)}, u32[]{:S(2)}) copy-start(f32[64]{0:T(128)} %param.13) | copy-start | bytes 772
  9.5 0.7 %copy-start.4 = (f32[64]{0:T(128)S(1)}, f32[64]{0:T(128)}, u32[]{:S(2)}) copy-start(f32[64]{0:T(128)} %param.15) | copy-start | bytes 772
  9.5 0.7 %copy-start.5 = (f32[64]{0:T(128)S(1)}, f32[64]{0:T(128)}, u32[]{:S(2)}) copy-start(f32[64]{0:T(128)} %param.17) | copy-start | bytes 772
  10.2 0.9 %copy-start.1 = (bf16[9,64,64]{2,1,0:T(8,128)(2,1)S(1)}, bf16[9,64,64]{2,1,0:T(8,128)(2,1)}, u32[]{:S(2)}) copy-start(bf16[9,64,64]{2,1,0:T(8,128)(2,1)} %k3_ref.1) | copy-start | bytes 221188

commit v3 on v2

--- a/solution.py
+++ b/solution.py
@@ -37,11 +37,31 @@
         self.lanes = 4 * chans
 
 
+def pack_kernel(left_ref, right_ref, out_ref):
+    rows, cols = left_ref.shape
+    left = left_ref[...]
+    edges = []
+    for first in (0, cols - 3):
+        lane, n = iota((cols, cols), 0), iota((cols, cols), 1)
+        pick = jnp.where(lane == first + n // rows, 1.0, 0.0).astype(BF16)
+        value = jnp.dot(left, pick, preferred_element_type=F32)
+        y, n = iota((rows, cols), 0), iota((rows, cols), 1)
+        value = jnp.where((y == n % rows) & (n < 3 * rows), value, 0.0)
+        edges.append(jnp.sum(value, axis=0, keepdims=True))
+    left = left.astype(F32)
+    message = jnp.concatenate(
+        [right_ref[...].astype(F32), left[:3], left[rows - 3 :]] + edges, axis=0
+    ).astype(BF16)
+    for k in range(out_ref.shape[0]):
+        out_ref[k] = message
+
+
 def prep_kernel(
-    plan, k1_ref, b1_ref, k2_ref, b2_ref, k3_ref, b3_ref, place_ref, list_ref,
-    w1_ref, w2_ref, w3_ref, b_ref, mask_ref, disp_ref, spread_ref,
+    plan, left_ref, k1_ref, b1_ref, k2_ref, b2_ref, k3_ref, b3_ref, place_ref, list_ref,
+    w1_ref, w2_ref, w3_ref, b_ref, mask_ref, disp_ref, spread_ref, own_ref,
 ):
     ch = plan.chans
+    own_ref[...] = left_ref[...].astype(F32)
     kernel = k1_ref[...]
     high = kernel.astype(BF16)
     rest = kernel - high.astype(F32)
@@ -110,31 +130,40 @@
 
 
 def main_kernel(
-    plan, place_ref, g_ref, spread_ref, w1_ref, b_ref, w2_ref, w3_ref, mask_at, disp_at, out_ref,
+    plan, place_ref, g_ref, left_ref, spread_ref, w1_ref, b_ref, w2_ref, w3_ref, mask_ref, disp_ref, out_ref,
     v_ref, v4_ref, fx_ref, f_ref, x1_ref, x2_ref, x3_ref, lb_ref, s_ref, tot_ref, mom_ref,
-    mask_ref, disp_ref, sems,
 ):
     rows, cols, ch = plan.rows, plan.cols, plan.chans
     row, col = place_ref[0], place_ref[1]
     first_row, last_row = row == 0, row == plan.n_row - 1
-    copies = [
-        pltpu.make_async_copy(source, target, sems.at[k])
-        for k, (source, target) in enumerate(((mask_at, mask_ref), (disp_at, disp_ref)))
-    ]
-    for copy in copies:
-        copy.start()
-
-    tiles = [(1, t if plan.ring else lax.rem(col + (t - 5 + plan.n_col), plan.n_col)) for t in range(plan.tiles)]
-    tiles += [(0, lax.rem(col + (t - 1 + plan.n_col), plan.n_col)) for t in range(3)]
-    for at, (image, tile) in enumerate(tiles):
+
+    def message(dr, tile):
+        return g_ref[jnp.clip(row + dr, 0, plan.n_row - 1) * plan.n_col + tile].astype(F32)
+
+    wide = plan.tiles * cols
+    for t in range(plan.tiles):
+        tile = t if plan.ring else lax.rem(col + (t - 5 + plan.n_col), plan.n_col)
         for dr in range(3):
-            source = jnp.clip(row + (dr - 1), 0, plan.n_row - 1) * plan.n_col + tile
-            v_ref[dr * rows : (dr + 1) * rows, at * cols : (at + 1) * cols] = g_ref[source, image].astype(F32)
+            v_ref[dr * rows : (dr + 1) * rows, t * cols : (t + 1) * cols] = message(dr - 1, tile)[:rows]
+    blank = jnp.zeros((rows - 3, cols), F32)
+    for t in range(3):
+        tile = lax.rem(col + (t - 1 + plan.n_col), plan.n_col)
+        at = slice(wide + t * cols, wide + (t + 1) * cols)
+        v_ref[0:rows, at] = jnp.concatenate([blank, message(-1, tile)[rows + 3 : rows + 6]], axis=0)
+        v_ref[2 * rows : 3 * rows, at] = jnp.concatenate([message(1, tile)[rows : rows + 3], blank], axis=0)
+        if t == 1:
+            v_ref[rows : 2 * rows, at] = left_ref[...]
+        else:
+            edge = jnp.broadcast_to(message(0, tile)[rows + (7 if t == 0 else 6) :][:1], (rows, cols))
+            y, n = iota((rows, cols), 0), iota((rows, cols), 1)
+            edge = jnp.where((y == n % rows) & (n < 3 * rows), edge, 0.0).astype(BF16)
+            n, lane = iota((cols, cols), 0), iota((cols, cols), 1)
+            pick = jnp.where((lane == (cols - 3 if t == 0 else 0) + n // rows) & (n < 3 * rows), 1.0, 0.0)
+            v_ref[rows : 2 * rows, at] = jnp.dot(edge, pick.astype(BF16), preferred_element_type=F32)
     for px in range(4):
         moved = v_ref[...] if px == 1 else pltpu.roll(v_ref[...], (1 - px) % v_ref.shape[1], 1)
         v4_ref[px * 64 : px * 64 + 3 * rows, :] = moved.astype(BF16)
         v4_ref[px * 64 + 3 * rows : px * 64 + 64, :] = jnp.zeros((64 - 3 * rows, v_ref.shape[1]), BF16)
-    wide = plan.tiles * cols
     seg_id = iota((SEGS, 1), 0)
     if plan.ring:
         begin = seg_id * plan.seg
@@ -311,8 +340,6 @@
     layer_three_left(0, 0)
     for u in range(chunks):
         layer_three(0, 0, u)
-    for copy in copies:
-        copy.wait()
 
     def together(j, top):
         for k in range(2):
@@ -349,10 +376,11 @@
         ch = kernel_one.shape[0]
         plan = Plan(mesh, rows, cols, ch)
         devices = plan.n_row * plan.n_col
-        images = jnp.stack([left_image, right_image])
-        gathered = lax.all_to_all(
-            jnp.broadcast_to(images, (devices,) + images.shape), ("row", "col"), 0, 0
-        )
+        message = pl.pallas_call(
+            pack_kernel,
+            out_shape=jax.ShapeDtypeStruct((devices, rows + 8, cols), BF16),
+        )(left_image, right_image)
+        gathered = lax.all_to_all(message, ("row", "col"), 0, 0)
         place = jnp.stack(
             [lax.axis_index("row"), lax.axis_index("col"), block_count[0, 0]]
         ).astype(jnp.int32)
@@ -360,7 +388,7 @@
         smem = pl.BlockSpec(memory_space=pltpu.SMEM)
         lanes = plan.lanes
         n_left = 4 * SEGS * plan.quads_left
-        w1, w2, w3, biases, mask, disp, spread = pl.pallas_call(
+        w1, w2, w3, biases, mask, disp, spread, own = pl.pallas_call(
             functools.partial(prep_kernel, plan),
             out_shape=(
                 jax.ShapeDtypeStruct((5, 256, lanes), BF16),
@@ -370,18 +398,19 @@
                 jax.ShapeDtypeStruct((plan.points, n_left), F32),
                 jax.ShapeDtypeStruct((plan.points, n_left), F32),
                 jax.ShapeDtypeStruct((256, 512), BF16),
+                jax.ShapeDtypeStruct((rows, cols), F32),
             ),
-            in_specs=[vmem] * 6 + [smem, smem],
-            out_specs=(vmem,) * 7,
+            in_specs=[vmem] * 7 + [smem, smem],
+            out_specs=(vmem,) * 8,
             compiler_params=pltpu.CompilerParams(vmem_limit_bytes=(12 if plan.ring else 24) * 2**20),
         )(
-            kernel_one.T, bias_one[None], kernel_two, bias_two[None], kernel_three, bias_three[None],
+            left_image, kernel_one.T, bias_one[None], kernel_two, bias_two[None], kernel_three, bias_three[None],
             place, block_list.reshape(-1),
         )
         return pl.pallas_call(
             functools.partial(main_kernel, plan),
             out_shape=jax.ShapeDtypeStruct((rows, cols), F32),
-            in_specs=[smem] + [vmem] * 6 + [pl.BlockSpec(memory_space=pltpu.HBM)] * 2,
+            in_specs=[smem] + [vmem] * 9,
             out_specs=vmem,
             scratch_shapes=[
                 pltpu.VMEM((3 * rows, (plan.tiles + 3) * cols), F32),
@@ -395,12 +424,9 @@
                 pltpu.VMEM((2, plan.points, 2 * n_left), F32),
                 pltpu.VMEM((rows + 4, cols), F32),
                 pltpu.VMEM((rows + 4, cols), F32),
-                pltpu.VMEM((plan.points, n_left), F32),
-                pltpu.VMEM((plan.points, n_left), F32),
-                pltpu.SemaphoreType.DMA((2,)),
             ],
             compiler_params=pltpu.CompilerParams(vmem_limit_bytes=(18 if plan.ring else 44) * 2**20),
-        )(place, gathered, spread, w1, biases, w2, w3, mask, disp)
+        )(place, gathered, own, spread, w1, biases, w2, w3, mask, disp)
 
     return jax.shard_map(
         per_device,

time: 33.5 us -> 31.9 us (0.952)
  Pallas kernels: 15.7 us -> 17.7 us
  local copies, waits for them, and re-layouts: 2.33 us -> 0.69 us
  waiting for transfers between devices: 6.37 us -> 5.17 us
  other arithmetic: 0.78 us -> 0.08 us
    pallas_call x0 -> x1, Pallas kernels: none -> 1.53 us  [per_device(): pl.pallas_call(pack_kernel, out_shape=jax.ShapeDtypeStruct((devices, rows...]
    all_to_all x1, waiting for transfers between devices: 6.37 us -> 5.17 us  [per_device(): gathered = lax.all_to_all(message, ('row', 'col'), 0, 0)]
    unnamed x14 -> x16, local copies, waits for them, and re-layouts: 1.6 us -> 0.69 us
    broadcast_in_dim x1 -> x0, local copies, waits for them, and re-layouts: 0.73 us -> none  [per_device(): jnp.broadcast_to(images, (devices,) + images.shape)]
    another operation x1 -> x0, other arithmetic: 0.71 us -> none  [per_device(): images = jnp.stack([left_image, right_image])]
    pallas_call x1, Pallas kernels: 13.7 us -> 14.2 us  [per_device(): pl.pallas_call(functools.partial(main_kernel, plan), out_shape=jax.ShapeD...]
where the time goes in v3:
time: 31.9 us; the launch traced here: 31.6 us
  Pallas kernels  17.7 us (55%)
  starting transfers between devices  7.3 us (23%)
  waiting for transfers between devices  5.17 us (16%)
  between operations  0.71 us (2%)
  local copies, waits for them, and re-layouts  0.69 us (2%)
    pallas_call x1, Pallas kernels, per_device(): pl.pallas_call(functools.partial(main_kernel, plan), out_shape=jax.ShapeD...  14.2 us
    all_to_all x1, starting transfers between devices, per_device(): gathered = lax.all_to_all(message, ('row', 'col'), 0, 0)  7.3 us
    all_to_all x1, waiting for transfers between devices, per_device(): gathered = lax.all_to_all(message, ('row', 'col'), 0, 0)  5.17 us
    pallas_call x1, Pallas kernels, per_device(): pl.pallas_call(functools.partial(prep_kernel, plan), out_shape=(jax.Shape...  1.91 us
    pallas_call x1, Pallas kernels, per_device(): pl.pallas_call(pack_kernel, out_shape=jax.ShapeDtypeStruct((devices, rows...  1.53 us
    unnamed x16, local copies, waits for them, and re-layouts  0.69 us
  transfers between devices with their start and end apart: 1, of which 1 were waited for; matrix products, arithmetic and copies ran while one was open for 0% of the time, Pallas kernels for 6%

profile of v3, /device:TPU:0, one launch (start us, length us, event | category | flops | bytes accessed | tf_op | source)
XLA Modules:
  0.0 31.6 jit_solution(3709617580421710542)
XLA Ops:
  0.0 1.5 %shard_map.100 = bf16[32,24,128]{2,1,0:T(8,128)(2,1)} custom-call(bf16[16,128]{1,0:T(8,128)(2,1)} %left_ref.3, bf16[16,128]{1,0:T(8,128)(2,1)} %right_ref.1), custom_call_target="tpu_custom_call" | custom-call | tf_op jit(solution)/shard_map/pallas_call | solution.py:379
  1.5 0.0 copy-start
  1.5 0.0 copy-start.1
  1.5 7.3 %all-to-all-start = ((bf16[32,24,128]{2,1,0:T(8,128)(2,1)}), bf16[32,24,128]{2,1,0:T(8,128)(2,1)S(1)}, u32[]{:S(2)}, u32[]{:S(2)}) async-start(bf16[32,24,128]{2,1,0:T(8,128)(2,1)} %shard_map.100), calls=%async_computation | async-start | bytes 393216 | tf_op jit(solution)/shard_map/all_to_all | solution.py:383
  9.5 0.0 copy-start.3
  9.5 0.1 pad_add_fusion.place_ref
  9.6 0.0 copy-start.7
  9.6 0.0 copy-start.2
  9.6 0.0 copy-start.4
  9.6 0.0 copy-start.5
  9.6 0.0 copy-start.6
  9.6 0.0 copy-done
  9.6 0.0 copy-done.1
  9.6 0.6 %copy-done.3 = f32[64,9]{0,1:T(8,128)S(1)} copy-done((f32[64,9]{0,1:T(8,128)S(1)}, f32[64,9]{0,1:T(8,128)}, u32[]{:S(2)}) %copy-start.3) | copy-done | bytes 2328
  10.2 0.0 copy-done.7
  10.2 0.0 copy-done.2
  10.3 0.0 copy-done.4
  10.3 0.0 copy-done.5
  10.3 0.0 copy-done.6
  10.3 1.9 %shard_map.101 = (bf16[5,256,256]{2,1,0:T(8,128)(2,1)S(1)}, bf16[1024,256]{1,0:T(8,128)(2,1)S(1)}, bf16[1024,256]{1,0:T(8,128)(2,1)S(1)}, f32[3,256]{1,0:T(4,128...) custom-call(bf16[16,128]{1,0:T(8,128)(2,1)S(1)} %copy-done.2, ...), custom_call_target="tpu_custom_call" | custom-call | tf_op jit(solution)/shard_map/pallas_call | solution.py:391
  12.2 5.2 %all-to-all-done.g_ref = bf16[32,24,128]{2,1,0:T(8,128)(2,1)S(1)} async-done(((bf16[32,24,128]{2,1,0:T(8,128)(2,1)}), bf16[32,24,128]{2,1,0:T(8,128)(2,1)S(1)}, u32[]{:S(2)}, u32[]{:S(2)}) %all-to-all-start) | async-done | bytes 196640 | tf_op jit(solution)/shard_map/all_to_all | solution.py:383
  17.4 14.2 %shard_map.102 = f32[16,128]{1,0:T(8,128)} custom-call(s32[3]{0:T(128)S(1)} %pad_add_fusion.place_ref, bf16[32,24,128]{2,1,0:T(8,128)(2,1)S(1)} %all-to-all-done.g_ref, f32[16,128]{1,0:T(8,128)S(1)} %get-tuple-element.13.left_ref, bf16[256,512]{1,0:T(8,128)(2,1)S(1)} %get-tuple-element.14.spread_ref, bf16[5,256,256]{2,1,0:T(8,128)(2,1)S(1)} %get-tuple-element.15.w1_ref, ...), custom_call_target="tpu_custom_call" | custom-call | tf_op jit(solution)/shard_map/pallas_call | solution.py:410
Async XLA Ops:
  1.5 8.1 %copy-start = (bf16[9,64,64]{2,1,0:T(8,128)(2,1)S(1)}, bf16[9,64,64]{2,1,0:T(8,128)(2,1)}, u32[]{:S(2)}) copy-start(bf16[9,64,64]{2,1,0:T(8,128)(2,1)} %k2_ref.1) | copy-start | bytes 221188
  1.5 8.1 %copy-start.1 = (bf16[9,64,64]{2,1,0:T(8,128)(2,1)S(1)}, bf16[9,64,64]{2,1,0:T(8,128)(2,1)}, u32[]{:S(2)}) copy-start(bf16[9,64,64]{2,1,0:T(8,128)(2,1)} %k3_ref.1) | copy-start | bytes 221188
  1.5 15.8 %all-to-all-start = ((bf16[32,24,128]{2,1,0:T(8,128)(2,1)}), bf16[32,24,128]{2,1,0:T(8,128)(2,1)S(1)}, u32[]{:S(2)}, u32[]{:S(2)}) async-start(bf16[32,24,128]{2,1,0:T(8,128)(2,1)} %shard_map.100), calls=%async_computation | async-start | bytes 393216 | tf_op jit(solution)/shard_map/all_to_all | solution.py:383
  9.5 0.7 %copy-start.3 = (f32[64,9]{0,1:T(8,128)S(1)}, f32[64,9]{0,1:T(8,128)}, u32[]{:S(2)}) copy-start(f32[64,9]{0,1:T(8,128)} %param.12) | copy-start | bytes 6916
  9.6 0.7 %copy-start.7 = (s32[1,1,8]{2,1,0:T(1,128)S(1)}, s32[1,1,8]{2,1,0:T(1,128)}, u32[]{:S(2)}) copy-start(s32[1,1,8]{2,1,0:T(1,128)} %param.18) | copy-start | bytes 100
  9.6 0.7 %copy-start.2 = (bf16[16,128]{1,0:T(8,128)(2,1)S(1)}, bf16[16,128]{1,0:T(8,128)(2,1)}, u32[]{:S(2)}) copy-start(bf16[16,128]{1,0:T(8,128)(2,1)} %left_ref.3) | copy-start | bytes 12292
  9.6 0.7 %copy-start.4 = (f32[64]{0:T(128)S(1)}, f32[64]{0:T(128)}, u32[]{:S(2)}) copy-start(f32[64]{0:T(128)} %param.13) | copy-start | bytes 772
  9.6 0.7 %copy-start.5 = (f32[64]{0:T(128)S(1)}, f32[64]{0:T(128)}, u32[]{:S(2)}) copy-start(f32[64]{0:T(128)} %param.15) | copy-start | bytes 772
  9.6 0.7 %copy-start.6 = (f32[64]{0:T(128)S(1)}, f32[64]{0:T(128)}, u32[]{:S(2)}) copy-start(f32[64]{0:T(128)} %param.17) | copy-start | bytes 772

commit v4 on v3

--- a/solution.py
+++ b/solution.py
@@ -218,7 +218,7 @@
             x1_ref[pl.ds(pl.multiple_of((5 * half + step) * pitch, SEGS), pitch)] = value.astype(BF16)
         return carry
 
-    lax.fori_loop(0, 2, layer_one, 0)
+    lax.fori_loop(0, 2, layer_one, 0, unroll=2)
 
     @pl.when(first_row)
     def _():
@@ -279,11 +279,14 @@
         )
 
     def layer_three(r, slot, u):
-        value = jnp.dot(patch(r, u * chunk, chunk), w3_ref[...], preferred_element_type=F32)
-        x3_ref[slot, u * chunk : (u + 1) * chunk] = (value + b_ref[2:3, :]).astype(BF16)
-
-    def layer_three_left(r, slot):
-        left = jnp.dot(patch(r, plan.left_at, per), w3_ref[...], preferred_element_type=F32) + b_ref[2:3, :]
+        rows_in = patch(r, u * chunk, chunk)
+        if u == 0:
+            rows_in = jnp.concatenate([rows_in, patch(r, plan.left_at, per)], axis=0)
+        value = jnp.dot(rows_in, w3_ref[...], preferred_element_type=F32) + b_ref[2:3, :]
+        x3_ref[slot, u * chunk : (u + 1) * chunk] = value[:chunk].astype(BF16)
+        if u:
+            return
+        left = value[chunk:]
         swapped = jnp.concatenate(
             [left[:, ch : 2 * ch], left[:, :ch], left[:, 3 * ch :], left[:, 2 * ch : 3 * ch]], axis=1
         )
@@ -337,14 +340,12 @@
                 target[pl.ds(2 * r + 2 + dy, 1), :] = value[:, :pair] + value[:, pair:]
 
     none = [jnp.zeros((8, 2 * pair), F32)] * 4
-    layer_three_left(0, 0)
     for u in range(chunks):
         layer_three(0, 0, u)
 
     def together(j, top):
         for k in range(2):
             state, later = none, None
-            layer_three_left(2 * j + k + 1, 1 - k)
             for u in range(chunks):
                 layer_three(2 * j + k + 1, 1 - k, u)
                 state = weigh(1 - k, u, top, state)
@@ -353,7 +354,7 @@
             top = spread_top(later)
         return top
 
-    top = lax.fori_loop(0, 4, together, jnp.zeros((8, 4 * pair), F32))
+    top = lax.fori_loop(0, 4, together, jnp.zeros((8, 4 * pair), F32), unroll=4)
     state = none
     for u in range(chunks):
         state = weigh(1, u, top, state)

time: 31.9 us -> 30.4 us (0.953)
  Pallas kernels: 17.7 us -> 16.1 us
    pallas_call x1, Pallas kernels: 14.2 us -> 12.7 us  [per_device(): pl.pallas_call(functools.partial(main_kernel, plan), out_shape=jax.ShapeD...]
where the time goes in v4:
time: 30.4 us; the launch traced here: 30.1 us
  Pallas kernels  16.1 us (53%)
  starting transfers between devices  7.3 us (24%)
  waiting for transfers between devices  5.17 us (17%)
  between operations  0.71 us (2%)
  local copies, waits for them, and re-layouts  0.69 us (2%)
    pallas_call x1, Pallas kernels, per_device(): pl.pallas_call(functools.partial(main_kernel, plan), out_shape=jax.ShapeD...  12.7 us
    all_to_all x1, starting transfers between devices, per_device(): gathered = lax.all_to_all(message, ('row', 'col'), 0, 0)  7.3 us
    all_to_all x1, waiting for transfers between devices, per_device(): gathered = lax.all_to_all(message, ('row', 'col'), 0, 0)  5.17 us
    pallas_call x1, Pallas kernels, per_device(): pl.pallas_call(functools.partial(prep_kernel, plan), out_shape=(jax.Shape...  1.91 us
    pallas_call x1, Pallas kernels, per_device(): pl.pallas_call(pack_kernel, out_shape=jax.ShapeDtypeStruct((devices, rows...  1.53 us
    unnamed x16, local copies, waits for them, and re-layouts  0.69 us
  transfers between devices with their start and end apart: 1, of which 1 were waited for; matrix products, arithmetic and copies ran while one was open for 0% of the time, Pallas kernels for 6%

profile of v4, /device:TPU:0, one launch (start us, length us, event | category | flops | bytes accessed | tf_op | source)
XLA Modules:
  0.0 30.1 jit_solution(1932721019795493616)
XLA Ops:
  0.0 1.5 %shard_map.100 = bf16[32,24,128]{2,1,0:T(8,128)(2,1)} custom-call(bf16[16,128]{1,0:T(8,128)(2,1)} %left_ref.3, bf16[16,128]{1,0:T(8,128)(2,1)} %right_ref.1), custom_call_target="tpu_custom_call" | custom-call | tf_op jit(solution)/shard_map/pallas_call | solution.py:380
  1.5 0.0 copy-start
  1.5 0.0 copy-start.1
  1.5 7.3 %all-to-all-start = ((bf16[32,24,128]{2,1,0:T(8,128)(2,1)}), bf16[32,24,128]{2,1,0:T(8,128)(2,1)S(1)}, u32[]{:S(2)}, u32[]{:S(2)}) async-start(bf16[32,24,128]{2,1,0:T(8,128)(2,1)} %shard_map.100), calls=%async_computation | async-start | bytes 393216 | tf_op jit(solution)/shard_map/all_to_all | solution.py:384
  9.5 0.0 copy-start.3
  9.5 0.1 pad_add_fusion.place_ref
  9.6 0.0 copy-start.7
  9.6 0.0 copy-start.2
  9.6 0.0 copy-start.4
  9.6 0.0 copy-start.5
  9.6 0.0 copy-start.6
  9.6 0.0 copy-done
  9.6 0.0 copy-done.1
  9.6 0.6 %copy-done.3 = f32[64,9]{0,1:T(8,128)S(1)} copy-done((f32[64,9]{0,1:T(8,128)S(1)}, f32[64,9]{0,1:T(8,128)}, u32[]{:S(2)}) %copy-start.3) | copy-done | bytes 2328
  10.2 0.0 copy-done.7
  10.2 0.0 copy-done.2
  10.3 0.0 copy-done.4
  10.3 0.0 copy-done.5
  10.3 0.0 copy-done.6
  10.3 1.9 %shard_map.101 = (bf16[5,256,256]{2,1,0:T(8,128)(2,1)S(1)}, bf16[1024,256]{1,0:T(8,128)(2,1)S(1)}, bf16[1024,256]{1,0:T(8,128)(2,1)S(1)}, f32[3,256]{1,0:T(4,128...) custom-call(bf16[16,128]{1,0:T(8,128)(2,1)S(1)} %copy-done.2, ...), custom_call_target="tpu_custom_call" | custom-call | tf_op jit(solution)/shard_map/pallas_call | solution.py:392
  12.2 5.2 %all-to-all-done.g_ref = bf16[32,24,128]{2,1,0:T(8,128)(2,1)S(1)} async-done(((bf16[32,24,128]{2,1,0:T(8,128)(2,1)}), bf16[32,24,128]{2,1,0:T(8,128)(2,1)S(1)}, u32[]{:S(2)}, u32[]{:S(2)}) %all-to-all-start) | async-done | bytes 196640 | tf_op jit(solution)/shard_map/all_to_all | solution.py:384
  17.4 12.7 %shard_map.102 = f32[16,128]{1,0:T(8,128)} custom-call(s32[3]{0:T(128)S(1)} %pad_add_fusion.place_ref, bf16[32,24,128]{2,1,0:T(8,128)(2,1)S(1)} %all-to-all-done.g_ref, f32[16,128]{1,0:T(8,128)S(1)} %get-tuple-element.13.left_ref, bf16[256,512]{1,0:T(8,128)(2,1)S(1)} %get-tuple-element.14.spread_ref, bf16[5,256,256]{2,1,0:T(8,128)(2,1)S(1)} %get-tuple-element.15.w1_ref, ...), custom_call_target="tpu_custom_call" | custom-call | tf_op jit(solution)/shard_map/pallas_call | solution.py:411
Async XLA Ops:
  1.5 8.1 %copy-start = (bf16[9,64,64]{2,1,0:T(8,128)(2,1)S(1)}, bf16[9,64,64]{2,1,0:T(8,128)(2,1)}, u32[]{:S(2)}) copy-start(bf16[9,64,64]{2,1,0:T(8,128)(2,1)} %k2_ref.1) | copy-start | bytes 221188
  1.5 8.1 %copy-start.1 = (bf16[9,64,64]{2,1,0:T(8,128)(2,1)S(1)}, bf16[9,64,64]{2,1,0:T(8,128)(2,1)}, u32[]{:S(2)}) copy-start(bf16[9,64,64]{2,1,0:T(8,128)(2,1)} %k3_ref.1) | copy-start | bytes 221188
  1.5 15.8 %all-to-all-start = ((bf16[32,24,128]{2,1,0:T(8,128)(2,1)}), bf16[32,24,128]{2,1,0:T(8,128)(2,1)S(1)}, u32[]{:S(2)}, u32[]{:S(2)}) async-start(bf16[32,24,128]{2,1,0:T(8,128)(2,1)} %shard_map.100), calls=%async_computation | async-start | bytes 393216 | tf_op jit(solution)/shard_map/all_to_all | solution.py:384
  9.5 0.7 %copy-start.3 = (f32[64,9]{0,1:T(8,128)S(1)}, f32[64,9]{0,1:T(8,128)}, u32[]{:S(2)}) copy-start(f32[64,9]{0,1:T(8,128)} %param.12) | copy-start | bytes 6916
  9.6 0.7 %copy-start.7 = (s32[1,1,8]{2,1,0:T(1,128)S(1)}, s32[1,1,8]{2,1,0:T(1,128)}, u32[]{:S(2)}) copy-start(s32[1,1,8]{2,1,0:T(1,128)} %param.18) | copy-start | bytes 100
  9.6 0.7 %copy-start.2 = (bf16[16,128]{1,0:T(8,128)(2,1)S(1)}, bf16[16,128]{1,0:T(8,128)(2,1)}, u32[]{:S(2)}) copy-start(bf16[16,128]{1,0:T(8,128)(2,1)} %left_ref.3) | copy-start | bytes 12292
  9.6 0.7 %copy-start.4 = (f32[64]{0:T(128)S(1)}, f32[64]{0:T(128)}, u32[]{:S(2)}) copy-start(f32[64]{0:T(128)} %param.13) | copy-start | bytes 772
  9.6 0.7 %copy-start.5 = (f32[64]{0:T(128)S(1)}, f32[64]{0:T(128)}, u32[]{:S(2)}) copy-start(f32[64]{0:T(128)} %param.15) | copy-start | bytes 772
  9.6 0.7 %copy-start.6 = (f32[64]{0:T(128)S(1)}, f32[64]{0:T(128)}, u32[]{:S(2)}) copy-start(f32[64]{0:T(128)} %param.17) | copy-start | bytes 772

commit v5 on v4

--- a/solution.py
+++ b/solution.py
@@ -211,56 +211,64 @@
 
     pitch = plan.total
 
-    def layer_one(half, carry):
-        for step in range(5):
-            value = jnp.dot(f_ref[half], w1_ref[step], preferred_element_type=F32)
-            value = clear_first(jax.nn.relu(value + b_ref[0:1, :]))
-            x1_ref[pl.ds(pl.multiple_of((5 * half + step) * pitch, SEGS), pitch)] = value.astype(BF16)
-        return carry
-
-    lax.fori_loop(0, 2, layer_one, 0, unroll=2)
-
-    @pl.when(first_row)
-    def _():
-        x1_ref[0:pitch] = jnp.zeros((pitch, plan.lanes), BF16)
-
-    @pl.when(last_row)
-    def _():
-        x1_ref[9 * pitch :] = jnp.zeros((pitch, plan.lanes), BF16)
-
-    def four(source, weight, start, count):
-        value = None
+    top_row = jnp.where(first_row, 0.0, 1.0).astype(F32)
+    end_row = jnp.where(last_row, 0.0, 1.0).astype(F32)
+    def layer_one(step):
+        value = jnp.dot(f_ref[step // 5], w1_ref[step % 5], preferred_element_type=F32)
+        value = clear_first(jax.nn.relu(value + b_ref[0:1, :]))
+        if step == 0:
+            value = value * top_row
+        if step == 9:
+            value = value * end_row
+        x1_ref[step * pitch : (step + 1) * pitch] = value.astype(BF16)
+
+
+    odd = (iota((SEGS, plan.lanes), 1) // ch) % 2
+
+    half_at = (plan.quads + 1) // 2 * SEGS + 3 * SEGS
+    right_end = (plan.quads + 1) * SEGS
+    left_end = plan.left_at + (plan.quads_left + 1) * SEGS
+
+    def patch_two(base, pieces):
+        parts = []
         for k in range(4):
-            at = pl.multiple_of(start + (k // 2) * pitch + (k % 2) * SEGS, SEGS)
-            part = jnp.dot(source[pl.ds(at, count)], weight[k * 256 : k * 256 + 256], preferred_element_type=F32)
-            value = part if value is None else value + part
-        return value
-
-    odd = (iota((SEGS, plan.lanes), 1) // ch) % 2
-
-    def layer_two(i, carry):
-        start = i * (3 * pitch)
-        value = four(x1_ref, w2_ref, start, 3 * pitch - SEGS)
-        value = jax.nn.relu(value + b_ref[1:2, :])
-        x2_ref[pl.ds(pl.multiple_of(start, SEGS), 3 * pitch - SEGS)] = value.astype(BF16)
-        for k in range(3):
-            for seg, at, edges in areas:
-                for low in (True, False):
-                    base = k * pitch + at + (0 if low else (seg // 2) * SEGS)
-                    piece = value[base : base + SEGS]
-                    piece = jnp.where(odd == (0 if low else 1), piece * edges[0 if low else 1], piece)
-                    x2_ref[pl.ds(pl.multiple_of(start + base, SEGS), SEGS)] = piece.astype(BF16)
-        return carry
-
-    lax.fori_loop(0, 3, layer_two, 0)
-
-    @pl.when(first_row)
-    def _():
-        x2_ref[0:pitch, 0 : 2 * ch] = jnp.zeros((pitch, 2 * ch), BF16)
-
-    @pl.when(last_row)
-    def _():
-        x2_ref[8 * pitch : 9 * pitch, 2 * ch :] = jnp.zeros((pitch, 2 * ch), BF16)
+            at = base + (k // 2) * pitch + (k % 2) * SEGS
+            part = [x1_ref[pl.ds(at + low, high - low)] for low, high in pieces]
+            parts.append(part[0] if len(part) == 1 else jnp.concatenate(part, axis=0))
+        return jnp.concatenate(parts, axis=1)
+
+    def layer_two(r, parts=(0, 1)):
+        base = r * pitch if isinstance(r, int) else pl.multiple_of(r * pitch, SEGS)
+        for pieces in [(((0, half_at),), ((half_at, right_end), (plan.left_at, left_end)))[p] for p in parts]:
+            value = jnp.dot(patch_two(base, pieces), w2_ref[...], preferred_element_type=F32)
+            value = jax.nn.relu(value + b_ref[1:2, :])
+            if isinstance(r, int) and r in (0, 8):
+                group_row = iota((1, plan.lanes), 1) // (2 * ch)
+                keep = jnp.where(group_row == r // 8, top_row if r == 0 else end_row, 1.0)
+                value = value * keep
+            start = 0
+            for low, high in pieces:
+                piece = value[start : start + high - low]
+                start += high - low
+                for (seg, at, edges) in areas:
+                    end = at + (seg // 2 + 1) * SEGS
+                    if low == at:
+                        first = piece[:SEGS]
+                        piece = jnp.concatenate([jnp.where(odd == 0, first * edges[0], first), piece[SEGS:]], axis=0)
+                    if high == end:
+                        last = piece[high - low - SEGS :]
+                        piece = jnp.concatenate(
+                            [piece[: high - low - SEGS], jnp.where(odd == 1, last * edges[1], last)], axis=0
+                        )
+                x2_ref[pl.ds(base + low, high - low)] = piece.astype(BF16)
+
+    for step in range(5):
+        layer_one(step)
+    for r in range(4):
+        if r + 5 < 10:
+            layer_one(r + 5)
+        layer_two(r)
+    layer_one(9)
 
     per = plan.quads_left * SEGS
     group = iota((per, plan.lanes), 1) // ch
@@ -337,34 +345,33 @@
         for dy in range(2):
             for target, value in ((tot_ref, state[2 * dy]), (mom_ref, state[2 * dy + 1])):
                 value = jnp.sum(value, axis=0, keepdims=True)
-                target[pl.ds(2 * r + 2 + dy, 1), :] = value[:, :pair] + value[:, pair:]
+                target[2 * r + dy : 2 * r + dy + 1, :] = value[:, :pair] + value[:, pair:]
 
     none = [jnp.zeros((8, 2 * pair), F32)] * 4
     for u in range(chunks):
         layer_three(0, 0, u)
 
-    def together(j, top):
-        for k in range(2):
-            state, later = none, None
-            for u in range(chunks):
-                layer_three(2 * j + k + 1, 1 - k, u)
-                state = weigh(1 - k, u, top, state)
-                later = multiply(k, u, later)
-            keep_sums(2 * j + k - 1, state)
-            top = spread_top(later)
-        return top
-
-    top = lax.fori_loop(0, 4, together, jnp.zeros((8, 4 * pair), F32), unroll=4)
-    state = none
-    for u in range(chunks):
-        state = weigh(1, u, top, state)
-    keep_sums(7, state)
+    top = None
+    for r in range(9):
+        slot, state, later = r % 2, none, None
+        for u in range(chunks):
+            if r + 4 < 9:
+                layer_two(r + 4, range(u * 2 // chunks, (u + 1) * 2 // chunks))
+            if r < 7:
+                layer_three(r + 1, 1 - slot, u)
+            if r > 0:
+                state = weigh(1 - slot, u, top, state)
+            if r < 8:
+                later = multiply(slot, u, later)
+        if r > 0:
+            keep_sums(r - 1, state)
+        top = spread_top(later) if r < 8 else None
 
     n, p = iota((pair, cols), 0), iota((pair, cols), 1)
     left = n % per
     place = (left % SEGS) * plan.seg_left + 2 * (left // SEGS) + n // per
     turn = jnp.where(place == p, 1.0, 0.0).astype(F32)
-    value = mom_ref[2 : rows + 2, :] / tot_ref[2 : rows + 2, :] * (1.0 / cols)
+    value = mom_ref[...] / tot_ref[...] * (1.0 / cols)
     out_ref[...] = jnp.dot(value, turn, precision=lax.Precision.HIGHEST, preferred_element_type=F32)
 
 
@@ -423,8 +430,8 @@
                 pltpu.VMEM((2, plan.points, lanes), BF16),
                 pltpu.VMEM((2, 2 * n_left, lanes), BF16),
                 pltpu.VMEM((2, plan.points, 2 * n_left), F32),
-                pltpu.VMEM((rows + 4, cols), F32),
-                pltpu.VMEM((rows + 4, cols), F32),
+                pltpu.VMEM((rows, cols), F32),
+                pltpu.VMEM((rows, cols), F32),
             ],
             compiler_params=pltpu.CompilerParams(vmem_limit_bytes=(18 if plan.ring else 44) * 2**20),
         )(place, gathered, own, spread, w1, biases, w2, w3, mask, disp)

time: 30.4 us -> 29.2 us (0.961)
  Pallas kernels: 16.1 us -> 15 us
    pallas_call x1, Pallas kernels: 12.7 us -> 11.5 us  [per_device(): pl.pallas_call(functools.partial(main_kernel, plan), out_shape=jax.ShapeD...]
  transfers between devices with their start and end apart: 1 -> 1, of which waited for: 1 -> 1; matrix products, arithmetic and copies ran while one was open for 0% -> 0% of each run, Pallas kernels for 6% -> 7%
where the time goes in v5:
time: 29.2 us; the launch traced here: 28.9 us
  Pallas kernels  15 us (51%)
  starting transfers between devices  7.3 us (25%)
  waiting for transfers between devices  5.17 us (18%)
  between operations  0.71 us (2%)
  local copies, waits for them, and re-layouts  0.69 us (2%)
    pallas_call x1, Pallas kernels, per_device(): pl.pallas_call(functools.partial(main_kernel, plan), out_shape=jax.ShapeD...  11.5 us
    all_to_all x1, starting transfers between devices, per_device(): gathered = lax.all_to_all(message, ('row', 'col'), 0, 0)  7.3 us
    all_to_all x1, waiting for transfers between devices, per_device(): gathered = lax.all_to_all(message, ('row', 'col'), 0, 0)  5.17 us
    pallas_call x1, Pallas kernels, per_device(): pl.pallas_call(functools.partial(prep_kernel, plan), out_shape=(jax.Shape...  1.91 us
    pallas_call x1, Pallas kernels, per_device(): pl.pallas_call(pack_kernel, out_shape=jax.ShapeDtypeStruct((devices, rows...  1.53 us
    unnamed x16, local copies, waits for them, and re-layouts  0.69 us
  transfers between devices with their start and end apart: 1, of which 1 were waited for; matrix products, arithmetic and copies ran while one was open for 0% of the time, Pallas kernels for 7%

profile of v5, /device:TPU:0, one launch (start us, length us, event | category | flops | bytes accessed | tf_op | source)
XLA Modules:
  0.0 28.9 jit_solution(4093667650736439264)
XLA Ops:
  0.0 1.5 %shard_map.100 = bf16[32,24,128]{2,1,0:T(8,128)(2,1)} custom-call(bf16[16,128]{1,0:T(8,128)(2,1)} %left_ref.3, bf16[16,128]{1,0:T(8,128)(2,1)} %right_ref.1), custom_call_target="tpu_custom_call" | custom-call | tf_op jit(solution)/shard_map/pallas_call | solution.py:387
  1.5 0.0 copy-start
  1.5 0.0 copy-start.1
  1.5 7.3 %all-to-all-start = ((bf16[32,24,128]{2,1,0:T(8,128)(2,1)}), bf16[32,24,128]{2,1,0:T(8,128)(2,1)S(1)}, u32[]{:S(2)}, u32[]{:S(2)}) async-start(bf16[32,24,128]{2,1,0:T(8,128)(2,1)} %shard_map.100), calls=%async_computation | async-start | bytes 393216 | tf_op jit(solution)/shard_map/all_to_all | solution.py:391
  9.5 0.0 copy-start.3
  9.5 0.1 pad_add_fusion.place_ref
  9.6 0.0 copy-start.7
  9.6 0.0 copy-start.2
  9.6 0.0 copy-start.4
  9.6 0.0 copy-start.5
  9.6 0.0 copy-start.6
  9.6 0.0 copy-done
  9.6 0.0 copy-done.1
  9.6 0.6 %copy-done.3 = f32[64,9]{0,1:T(8,128)S(1)} copy-done((f32[64,9]{0,1:T(8,128)S(1)}, f32[64,9]{0,1:T(8,128)}, u32[]{:S(2)}) %copy-start.3) | copy-done | bytes 2328
  10.2 0.0 copy-done.7
  10.2 0.0 copy-done.2
  10.3 0.0 copy-done.4
  10.3 0.0 copy-done.5
  10.3 0.0 copy-done.6
  10.3 1.9 %shard_map.101 = (bf16[5,256,256]{2,1,0:T(8,128)(2,1)S(1)}, bf16[1024,256]{1,0:T(8,128)(2,1)S(1)}, bf16[1024,256]{1,0:T(8,128)(2,1)S(1)}, f32[3,256]{1,0:T(4,128...) custom-call(bf16[16,128]{1,0:T(8,128)(2,1)S(1)} %copy-done.2, ...), custom_call_target="tpu_custom_call" | custom-call | tf_op jit(solution)/shard_map/pallas_call | solution.py:399
  12.2 5.2 %all-to-all-done.g_ref = bf16[32,24,128]{2,1,0:T(8,128)(2,1)S(1)} async-done(((bf16[32,24,128]{2,1,0:T(8,128)(2,1)}), bf16[32,24,128]{2,1,0:T(8,128)(2,1)S(1)}, u32[]{:S(2)}, u32[]{:S(2)}) %all-to-all-start) | async-done | bytes 196640 | tf_op jit(solution)/shard_map/all_to_all | solution.py:391
  17.4 11.5 %shard_map.102 = f32[16,128]{1,0:T(8,128)} custom-call(s32[3]{0:T(128)S(1)} %pad_add_fusion.place_ref, bf16[32,24,128]{2,1,0:T(8,128)(2,1)S(1)} %all-to-all-done.g_ref, f32[16,128]{1,0:T(8,128)S(1)} %get-tuple-element.13.left_ref, bf16[256,512]{1,0:T(8,128)(2,1)S(1)} %get-tuple-element.14.spread_ref, bf16[5,256,256]{2,1,0:T(8,128)(2,1)S(1)} %get-tuple-element.15.w1_ref, ...), custom_call_target="tpu_custom_call" | custom-call | tf_op jit(solution)/shard_map/pallas_call | solution.py:418
Async XLA Ops:
  1.5 8.1 %copy-start = (bf16[9,64,64]{2,1,0:T(8,128)(2,1)S(1)}, bf16[9,64,64]{2,1,0:T(8,128)(2,1)}, u32[]{:S(2)}) copy-start(bf16[9,64,64]{2,1,0:T(8,128)(2,1)} %k2_ref.1) | copy-start | bytes 221188
  1.5 8.1 %copy-start.1 = (bf16[9,64,64]{2,1,0:T(8,128)(2,1)S(1)}, bf16[9,64,64]{2,1,0:T(8,128)(2,1)}, u32[]{:S(2)}) copy-start(bf16[9,64,64]{2,1,0:T(8,128)(2,1)} %k3_ref.1) | copy-start | bytes 221188
  1.5 15.8 %all-to-all-start = ((bf16[32,24,128]{2,1,0:T(8,128)(2,1)}), bf16[32,24,128]{2,1,0:T(8,128)(2,1)S(1)}, u32[]{:S(2)}, u32[]{:S(2)}) async-start(bf16[32,24,128]{2,1,0:T(8,128)(2,1)} %shard_map.100), calls=%async_computation | async-start | bytes 393216 | tf_op jit(solution)/shard_map/all_to_all | solution.py:391
  9.5 0.7 %copy-start.3 = (f32[64,9]{0,1:T(8,128)S(1)}, f32[64,9]{0,1:T(8,128)}, u32[]{:S(2)}) copy-start(f32[64,9]{0,1:T(8,128)} %param.12) | copy-start | bytes 6916
  9.6 0.7 %copy-start.7 = (s32[1,1,8]{2,1,0:T(1,128)S(1)}, s32[1,1,8]{2,1,0:T(1,128)}, u32[]{:S(2)}) copy-start(s32[1,1,8]{2,1,0:T(1,128)} %param.18) | copy-start | bytes 100
  9.6 0.7 %copy-start.2 = (bf16[16,128]{1,0:T(8,128)(2,1)S(1)}, bf16[16,128]{1,0:T(8,128)(2,1)}, u32[]{:S(2)}) copy-start(bf16[16,128]{1,0:T(8,128)(2,1)} %left_ref.3) | copy-start | bytes 12292
  9.6 0.7 %copy-start.4 = (f32[64]{0:T(128)S(1)}, f32[64]{0:T(128)}, u32[]{:S(2)}) copy-start(f32[64]{0:T(128)} %param.13) | copy-start | bytes 772
  9.6 0.7 %copy-start.5 = (f32[64]{0:T(128)S(1)}, f32[64]{0:T(128)}, u32[]{:S(2)}) copy-start(f32[64]{0:T(128)} %param.15) | copy-start | bytes 772
  9.6 0.7 %copy-start.6 = (f32[64]{0:T(128)S(1)}, f32[64]{0:T(128)}, u32[]{:S(2)}) copy-start(f32[64]{0:T(128)} %param.17) | copy-start | bytes 772

commit v6 on v5

--- a/solution.py
+++ b/solution.py
@@ -57,7 +57,7 @@
 
 
 def prep_kernel(
-    plan, left_ref, k1_ref, b1_ref, k2_ref, b2_ref, k3_ref, b3_ref, place_ref, list_ref,
+    plan, left_ref, k1_ref, b1_ref, k2_ref, b2_ref, k3_ref, b3_ref, list_ref, count_ref,
     w1_ref, w2_ref, w3_ref, b_ref, mask_ref, disp_ref, spread_ref, own_ref,
 ):
     ch = plan.chans
@@ -96,10 +96,10 @@
                 quad, sub = (py // 2) * 2 + px // 2, (py % 2) * 2 + px % 2
                 at = (4 * quad + sub) * ch
                 target[at : at + ch, :] = jnp.concatenate(pieces, axis=1).astype(BF16)
-    col = place_ref[1]
+    col = lax.axis_index("col")
     bits = jnp.int32(0)
     for k in range(list_ref.shape[0]):
-        bits = bits | jnp.where(k < place_ref[2], jnp.left_shift(jnp.int32(1), list_ref[k]), 0)
+        bits = bits | jnp.where(k < count_ref[0], jnp.left_shift(jnp.int32(1), list_ref[k]), 0)
     reach = SPAN * plan.cols
     shape = (plan.points, 4 * SEGS * plan.quads_left)
     m, n = iota(shape, 0), iota(shape, 1)
@@ -120,7 +120,7 @@
     mask_ref[...] = jnp.where(listed > 0, 0.0, -1e30).astype(F32)
     disp_ref[...] = d.astype(F32)
 
-    row = place_ref[0]
+    row = lax.axis_index("row")
     k, n = iota((256, 1), 0), iota((1, 512), 1)
     y = 10 * (n // 256) + n % 16
     wanted = jnp.where((y < plan.rows + 6) & (n % 256 < 192), (n // 16) % 4 * 64 + plan.rows - 3 + y, -1)
@@ -130,11 +130,11 @@
 
 
 def main_kernel(
-    plan, place_ref, g_ref, left_ref, spread_ref, w1_ref, b_ref, w2_ref, w3_ref, mask_ref, disp_ref, out_ref,
+    plan, g_ref, left_ref, spread_ref, w1_ref, b_ref, w2_ref, w3_ref, mask_ref, disp_ref, out_ref,
     v_ref, v4_ref, fx_ref, f_ref, x1_ref, x2_ref, x3_ref, lb_ref, s_ref, tot_ref, mom_ref,
 ):
     rows, cols, ch = plan.rows, plan.cols, plan.chans
-    row, col = place_ref[0], place_ref[1]
+    row, col = lax.axis_index("row"), lax.axis_index("col")
     first_row, last_row = row == 0, row == plan.n_row - 1
 
     def message(dr, tile):
@@ -145,25 +145,6 @@
         tile = t if plan.ring else lax.rem(col + (t - 5 + plan.n_col), plan.n_col)
         for dr in range(3):
             v_ref[dr * rows : (dr + 1) * rows, t * cols : (t + 1) * cols] = message(dr - 1, tile)[:rows]
-    blank = jnp.zeros((rows - 3, cols), F32)
-    for t in range(3):
-        tile = lax.rem(col + (t - 1 + plan.n_col), plan.n_col)
-        at = slice(wide + t * cols, wide + (t + 1) * cols)
-        v_ref[0:rows, at] = jnp.concatenate([blank, message(-1, tile)[rows + 3 : rows + 6]], axis=0)
-        v_ref[2 * rows : 3 * rows, at] = jnp.concatenate([message(1, tile)[rows : rows + 3], blank], axis=0)
-        if t == 1:
-            v_ref[rows : 2 * rows, at] = left_ref[...]
-        else:
-            edge = jnp.broadcast_to(message(0, tile)[rows + (7 if t == 0 else 6) :][:1], (rows, cols))
-            y, n = iota((rows, cols), 0), iota((rows, cols), 1)
-            edge = jnp.where((y == n % rows) & (n < 3 * rows), edge, 0.0).astype(BF16)
-            n, lane = iota((cols, cols), 0), iota((cols, cols), 1)
-            pick = jnp.where((lane == (cols - 3 if t == 0 else 0) + n // rows) & (n < 3 * rows), 1.0, 0.0)
-            v_ref[rows : 2 * rows, at] = jnp.dot(edge, pick.astype(BF16), preferred_element_type=F32)
-    for px in range(4):
-        moved = v_ref[...] if px == 1 else pltpu.roll(v_ref[...], (1 - px) % v_ref.shape[1], 1)
-        v4_ref[px * 64 : px * 64 + 3 * rows, :] = moved.astype(BF16)
-        v4_ref[px * 64 + 3 * rows : px * 64 + 64, :] = jnp.zeros((64 - 3 * rows, v_ref.shape[1]), BF16)
     seg_id = iota((SEGS, 1), 0)
     if plan.ring:
         begin = seg_id * plan.seg
@@ -182,7 +163,14 @@
         (plan.seg_left, plan.left_at, edges_left),
     )
     px_lane = iota((SEGS, 256), 1) // 64
-    for start, before, size, (seg, at, edges) in ((0, 0, wide, areas[0]), (wide, cols, 3 * cols, areas[1])):
+
+    def patches(start, before, size, area):
+        seg, at, edges = area
+        for px in range(4):
+            moved = v_ref[:, start : start + size]
+            moved = moved if px == 1 else pltpu.roll(moved, (1 - px) % size, 1)
+            v4_ref[px * 64 : px * 64 + 3 * rows, start : start + size] = moved.astype(BF16)
+            v4_ref[px * 64 + 3 * rows : px * 64 + 64, start : start + size] = jnp.zeros((64 - 3 * rows, size), BF16)
         count = (seg // 2 + 2) * SEGS
         n, k = iota((count, 1), 0), iota((1, size), 1)
         pick = jnp.where(before + (n % SEGS) * seg + 2 * (n // SEGS) - 2 == k, 1.0, 0.0).astype(BF16)
@@ -194,6 +182,24 @@
         fx_ref[at + count - 2 * SEGS : at + count - SEGS, :] = jnp.where(
             px_lane == 3, high * edges[1], high
         ).astype(BF16)
+
+    patches(0, 0, wide, areas[0])
+    blank = jnp.zeros((rows - 3, cols), F32)
+    for t in range(3):
+        tile = lax.rem(col + (t - 1 + plan.n_col), plan.n_col)
+        at = slice(wide + t * cols, wide + (t + 1) * cols)
+        v_ref[0:rows, at] = jnp.concatenate([blank, message(-1, tile)[rows + 3 : rows + 6]], axis=0)
+        v_ref[2 * rows : 3 * rows, at] = jnp.concatenate([message(1, tile)[rows : rows + 3], blank], axis=0)
+        if t == 1:
+            v_ref[rows : 2 * rows, at] = left_ref[...]
+        else:
+            edge = jnp.broadcast_to(message(0, tile)[rows + (7 if t == 0 else 6) :][:1], (rows, cols))
+            y, n = iota((rows, cols), 0), iota((rows, cols), 1)
+            edge = jnp.where((y == n % rows) & (n < 3 * rows), edge, 0.0).astype(BF16)
+            n, lane = iota((cols, cols), 0), iota((cols, cols), 1)
+            pick = jnp.where((lane == (cols - 3 if t == 0 else 0) + n // rows) & (n < 3 * rows), 1.0, 0.0)
+            v_ref[rows : 2 * rows, at] = jnp.dot(edge, pick.astype(BF16), preferred_element_type=F32)
+    patches(wide, cols, 3 * cols, areas[1])
     for half in range(2):
         value = jnp.dot(
             fx_ref[...], spread_ref[:, half * 256 : half * 256 + 256], preferred_element_type=F32
@@ -357,10 +363,10 @@
         for u in range(chunks):
             if r + 4 < 9:
                 layer_two(r + 4, range(u * 2 // chunks, (u + 1) * 2 // chunks))
+            if r > 0:
+                state = weigh(1 - slot, u, top, state)
             if r < 7:
                 layer_three(r + 1, 1 - slot, u)
-            if r > 0:
-                state = weigh(1 - slot, u, top, state)
             if r < 8:
                 later = multiply(slot, u, later)
         if r > 0:
@@ -389,9 +395,6 @@
             out_shape=jax.ShapeDtypeStruct((devices, rows + 8, cols), BF16),
         )(left_image, right_image)
         gathered = lax.all_to_all(message, ("row", "col"), 0, 0)
-        place = jnp.stack(
-            [lax.axis_index("row"), lax.axis_index("col"), block_count[0, 0]]
-        ).astype(jnp.int32)
         vmem = pl.BlockSpec(memory_space=pltpu.VMEM)
         smem = pl.BlockSpec(memory_space=pltpu.SMEM)
         lanes = plan.lanes
@@ -413,12 +416,12 @@
             compiler_params=pltpu.CompilerParams(vmem_limit_bytes=(12 if plan.ring else 24) * 2**20),
         )(
             left_image, kernel_one.T, bias_one[None], kernel_two, bias_two[None], kernel_three, bias_three[None],
-            place, block_list.reshape(-1),
+            block_list.reshape(-1), block_count.reshape(-1),
         )
         return pl.pallas_call(
             functools.partial(main_kernel, plan),
             out_shape=jax.ShapeDtypeStruct((rows, cols), F32),
-            in_specs=[smem] + [vmem] * 9,
+            in_specs=[vmem] * 9,
             out_specs=vmem,
             scratch_shapes=[
                 pltpu.VMEM((3 * rows, (plan.tiles + 3) * cols), F32),
@@ -434,7 +437,7 @@
                 pltpu.VMEM((rows, cols), F32),
             ],
             compiler_params=pltpu.CompilerParams(vmem_limit_bytes=(18 if plan.ring else 44) * 2**20),
-        )(place, gathered, own, spread, w1, biases, w2, w3, mask, disp)
+        )(gathered, own, spread, w1, biases, w2, w3, mask, disp)
 
     return jax.shard_map(
         per_device,

time: 29.2 us -> 28.2 us (0.966)
  Pallas kernels: 15 us -> 13.9 us
    pallas_call x1, Pallas kernels: 11.5 us -> 10.4 us  [per_device(): pl.pallas_call(functools.partial(main_kernel, plan), out_shape=jax.ShapeD...]
where the time goes in v6:
time: 28.2 us; the launch traced here: 27.8 us
  Pallas kernels  13.9 us (49%)
  starting transfers between devices  7.3 us (26%)
  waiting for transfers between devices  5.26 us (19%)
  between operations  0.76 us (3%)
  local copies, waits for them, and re-layouts  0.64 us (2%)
    pallas_call x1, Pallas kernels, per_device(): pl.pallas_call(functools.partial(main_kernel, plan), out_shape=jax.ShapeD...  10.4 us
    all_to_all x1, starting transfers between devices, per_device(): gathered = lax.all_to_all(message, ('row', 'col'), 0, 0)  7.3 us
    all_to_all x1, waiting for transfers between devices, per_device(): gathered = lax.all_to_all(message, ('row', 'col'), 0, 0)  5.26 us
    pallas_call x1, Pallas kernels, per_device(): pl.pallas_call(functools.partial(prep_kernel, plan), out_shape=(jax.Shape...  1.9 us
    pallas_call x1, Pallas kernels, per_device(): pl.pallas_call(pack_kernel, out_shape=jax.ShapeDtypeStruct((devices, rows...  1.53 us
    unnamed x16, local copies, waits for them, and re-layouts  0.64 us
  transfers between devices with their start and end apart: 1, of which 1 were waited for; matrix products, arithmetic and copies ran while one was open for 0% of the time, Pallas kernels for 7%

profile of v6, /device:TPU:0, one launch (start us, length us, event | category | flops | bytes accessed | tf_op | source)
XLA Modules:
  0.0 27.8 jit_solution(6300085056492363837)
XLA Ops:
  0.0 1.5 %shard_map.100 = bf16[32,24,128]{2,1,0:T(8,128)(2,1)} custom-call(bf16[16,128]{1,0:T(8,128)(2,1)} %left_ref.3, bf16[16,128]{1,0:T(8,128)(2,1)} %right_ref.1), custom_call_target="tpu_custom_call" | custom-call | tf_op jit(solution)/shard_map/pallas_call | solution.py:393
  1.5 0.0 copy-start
  1.5 0.0 copy-start.1
  1.5 0.0 copy-start.6
  1.5 0.0 copy-start.7
  1.5 7.3 %all-to-all-start = ((bf16[32,24,128]{2,1,0:T(8,128)(2,1)}), bf16[32,24,128]{2,1,0:T(8,128)(2,1)S(1)}, u32[]{:S(2)}, u32[]{:S(2)}) async-start(bf16[32,24,128]{2,1,0:T(8,128)(2,1)} %shard_map.100), calls=%async_computation | async-start | bytes 393216 | tf_op jit(solution)/shard_map/all_to_all | solution.py:397
  8.9 0.0 copy-start.3
  9.5 0.0 copy-start.2
  9.5 0.0 copy-start.4
  9.6 0.0 copy-start.5
  9.6 0.0 copy-done
  9.6 0.0 copy-done.1
  9.6 0.0 copy-done.6
  9.6 0.0 copy-done.7
  9.6 0.0 copy-done.3
  9.6 0.6 %copy-done.2 = bf16[16,128]{1,0:T(8,128)(2,1)S(1)} copy-done((bf16[16,128]{1,0:T(8,128)(2,1)S(1)}, bf16[16,128]{1,0:T(8,128)(2,1)}, u32[]{:S(2)}) %copy-start.2) | copy-done | bytes 4120
  10.2 0.0 copy-done.4
  10.2 0.0 copy-done.5
  10.2 1.9 %shard_map.101 = (bf16[5,256,256]{2,1,0:T(8,128)(2,1)S(1)}, bf16[1024,256]{1,0:T(8,128)(2,1)S(1)}, bf16[1024,256]{1,0:T(8,128)(2,1)S(1)}, f32[3,256]{1,0:T(4,128...) custom-call(bf16[16,128]{1,0:T(8,128)(2,1)S(1)} %copy-done.2, ...), custom_call_target="tpu_custom_call" | custom-call | tf_op jit(solution)/shard_map/pallas_call | solution.py:402
  12.1 5.3 %all-to-all-done.g_ref = bf16[32,24,128]{2,1,0:T(8,128)(2,1)S(1)} async-done(((bf16[32,24,128]{2,1,0:T(8,128)(2,1)}), bf16[32,24,128]{2,1,0:T(8,128)(2,1)S(1)}, u32[]{:S(2)}, u32[]{:S(2)}) %all-to-all-start) | async-done | bytes 196640 | tf_op jit(solution)/shard_map/all_to_all | solution.py:397
  17.4 10.4 %shard_map.102 = f32[16,128]{1,0:T(8,128)} custom-call(bf16[32,24,128]{2,1,0:T(8,128)(2,1)S(1)} %all-to-all-done.g_ref, f32[16,128]{1,0:T(8,128)S(1)} %get-tuple-element.13.left_ref, bf16[256,512]{1,0:T(8,128)(2,1)S(1)} %get-tuple-element.14.spread_ref, bf16[5,256,256]{2,1,0:T(8,128)(2,1)S(1)} %get-tuple-element.15.w1_ref, ...), custom_call_target="tpu_custom_call" | custom-call | tf_op jit(solution)/shard_map/pallas_call | solution.py:421
Async XLA Ops:
  1.5 8.0 %copy-start = (bf16[9,64,64]{2,1,0:T(8,128)(2,1)S(1)}, bf16[9,64,64]{2,1,0:T(8,128)(2,1)}, u32[]{:S(2)}) copy-start(bf16[9,64,64]{2,1,0:T(8,128)(2,1)} %k2_ref.1) | copy-start | bytes 221188
  1.5 8.0 %copy-start.1 = (bf16[9,64,64]{2,1,0:T(8,128)(2,1)S(1)}, bf16[9,64,64]{2,1,0:T(8,128)(2,1)}, u32[]{:S(2)}) copy-start(bf16[9,64,64]{2,1,0:T(8,128)(2,1)} %k3_ref.1) | copy-start | bytes 221188
  1.5 8.0 %copy-start.6 = (f32[64]{0:T(128)S(1)}, f32[64]{0:T(128)}, u32[]{:S(2)}) copy-start(f32[64]{0:T(128)} %param.17) | copy-start | bytes 772
  1.5 8.1 %copy-start.7 = (s32[1,1,8]{2,1,0:T(1,128)S(1)}, s32[1,1,8]{2,1,0:T(1,128)}, u32[]{:S(2)}) copy-start(s32[1,1,8]{2,1,0:T(1,128)} %param.18) | copy-start | bytes 100
  1.5 15.9 %all-to-all-start = ((bf16[32,24,128]{2,1,0:T(8,128)(2,1)}), bf16[32,24,128]{2,1,0:T(8,128)(2,1)S(1)}, u32[]{:S(2)}, u32[]{:S(2)}) async-start(bf16[32,24,128]{2,1,0:T(8,128)(2,1)} %shard_map.100), calls=%async_computation | async-start | bytes 393216 | tf_op jit(solution)/shard_map/all_to_all | solution.py:397
  8.9 0.7 %copy-start.3 = (f32[64,9]{0,1:T(8,128)S(1)}, f32[64,9]{0,1:T(8,128)}, u32[]{:S(2)}) copy-start(f32[64,9]{0,1:T(8,128)} %param.12) | copy-start | bytes 6916
  9.5 0.7 %copy-start.2 = (bf16[16,128]{1,0:T(8,128)(2,1)S(1)}, bf16[16,128]{1,0:T(8,128)(2,1)}, u32[]{:S(2)}) copy-start(bf16[16,128]{1,0:T(8,128)(2,1)} %left_ref.3) | copy-start | bytes 12292
  9.5 0.7 %copy-start.4 = (f32[64]{0:T(128)S(1)}, f32[64]{0:T(128)}, u32[]{:S(2)}) copy-start(f32[64]{0:T(128)} %param.13) | copy-start | bytes 772
  9.6 0.7 %copy-start.5 = (f32[64]{0:T(128)S(1)}, f32[64]{0:T(128)}, u32[]{:S(2)}) copy-start(f32[64]{0:T(128)} %param.15) | copy-start | bytes 772

commit v7 on v6

--- a/solution.py
+++ b/solution.py
@@ -200,11 +200,13 @@
             pick = jnp.where((lane == (cols - 3 if t == 0 else 0) + n // rows) & (n < 3 * rows), 1.0, 0.0)
             v_ref[rows : 2 * rows, at] = jnp.dot(edge, pick.astype(BF16), preferred_element_type=F32)
     patches(wide, cols, 3 * cols, areas[1])
-    for half in range(2):
+    def spread_half(half):
         value = jnp.dot(
             fx_ref[...], spread_ref[:, half * 256 : half * 256 + 256], preferred_element_type=F32
         )
         f_ref[half] = value.astype(BF16)
+
+    spread_half(0)
 
     def clear_first(value):
         pieces = []
@@ -270,6 +272,8 @@
 
     for step in range(5):
         layer_one(step)
+        if step == 1:
+            spread_half(1)
     for r in range(4):
         if r + 5 < 10:
             layer_one(r + 5)
@@ -357,6 +361,10 @@
     for u in range(chunks):
         layer_three(0, 0, u)
 
+    n, p = iota((pair, cols), 0), iota((pair, cols), 1)
+    left = n % per
+    place = (left % SEGS) * plan.seg_left + 2 * (left // SEGS) + n // per
+    turn = jnp.where(place == p, 1.0, 0.0).astype(BF16)
     top = None
     for r in range(9):
         slot, state, later = r % 2, none, None
@@ -373,12 +381,13 @@
             keep_sums(r - 1, state)
         top = spread_top(later) if r < 8 else None
 
-    n, p = iota((pair, cols), 0), iota((pair, cols), 1)
-    left = n % per
-    place = (left % SEGS) * plan.seg_left + 2 * (left // SEGS) + n // per
-    turn = jnp.where(place == p, 1.0, 0.0).astype(F32)
     value = mom_ref[...] / tot_ref[...] * (1.0 / cols)
-    out_ref[...] = jnp.dot(value, turn, precision=lax.Precision.HIGHEST, preferred_element_type=F32)
+    high = value.astype(BF16)
+    rest = value - high.astype(F32)
+    middle = rest.astype(BF16)
+    low = (rest - middle.astype(F32)).astype(BF16)
+    parts = jnp.concatenate([high, middle, low], axis=1)
+    out_ref[...] = jnp.dot(parts, jnp.concatenate([turn] * 3, axis=0), preferred_element_type=F32)
 
 
 def solution(mesh):

time: 28.2 us -> 28 us (level)
  no operation moved by 1% of the time
where the time goes in v7:
time: 28 us; the launch traced here: 27.7 us
  Pallas kernels  13.7 us (49%)
  starting transfers between devices  7.3 us (26%)
  waiting for transfers between devices  5.26 us (19%)
  between operations  0.76 us (3%)
  local copies, waits for them, and re-layouts  0.64 us (2%)
    pallas_call x1, Pallas kernels, per_device(): pl.pallas_call(functools.partial(main_kernel, plan), out_shape=jax.ShapeD...  10.3 us
    all_to_all x1, starting transfers between devices, per_device(): gathered = lax.all_to_all(message, ('row', 'col'), 0, 0)  7.3 us
    all_to_all x1, waiting for transfers between devices, per_device(): gathered = lax.all_to_all(message, ('row', 'col'), 0, 0)  5.26 us
    pallas_call x1, Pallas kernels, per_device(): pl.pallas_call(functools.partial(prep_kernel, plan), out_shape=(jax.Shape...  1.9 us
    pallas_call x1, Pallas kernels, per_device(): pl.pallas_call(pack_kernel, out_shape=jax.ShapeDtypeStruct((devices, rows...  1.53 us
    unnamed x16, local copies, waits for them, and re-layouts  0.64 us
  transfers between devices with their start and end apart: 1, of which 1 were waited for; matrix products, arithmetic and copies ran while one was open for 0% of the time, Pallas kernels for 7%

profile of v7, /device:TPU:0, one launch (start us, length us, event | category | flops | bytes accessed | tf_op | source)
XLA Modules:
  0.0 27.7 jit_solution(15184580180106658068)
XLA Ops:
  0.0 1.5 %shard_map.100 = bf16[32,24,128]{2,1,0:T(8,128)(2,1)} custom-call(bf16[16,128]{1,0:T(8,128)(2,1)} %left_ref.3, bf16[16,128]{1,0:T(8,128)(2,1)} %right_ref.1), custom_call_target="tpu_custom_call" | custom-call | tf_op jit(solution)/shard_map/pallas_call | solution.py:402
  1.5 0.0 copy-start
  1.5 0.0 copy-start.1
  1.5 0.0 copy-start.6
  1.5 0.0 copy-start.7
  1.5 7.3 %all-to-all-start = ((bf16[32,24,128]{2,1,0:T(8,128)(2,1)}), bf16[32,24,128]{2,1,0:T(8,128)(2,1)S(1)}, u32[]{:S(2)}, u32[]{:S(2)}) async-start(bf16[32,24,128]{2,1,0:T(8,128)(2,1)} %shard_map.100), calls=%async_computation | async-start | bytes 393216 | tf_op jit(solution)/shard_map/all_to_all | solution.py:406
  8.9 0.0 copy-start.3
  9.5 0.0 copy-start.2
  9.5 0.0 copy-start.4
  9.6 0.0 copy-start.5
  9.6 0.0 copy-done
  9.6 0.0 copy-done.1
  9.6 0.0 copy-done.6
  9.6 0.0 copy-done.7
  9.6 0.0 copy-done.3
  9.6 0.6 %copy-done.2 = bf16[16,128]{1,0:T(8,128)(2,1)S(1)} copy-done((bf16[16,128]{1,0:T(8,128)(2,1)S(1)}, bf16[16,128]{1,0:T(8,128)(2,1)}, u32[]{:S(2)}) %copy-start.2) | copy-done | bytes 4120
  10.2 0.0 copy-done.4
  10.2 0.0 copy-done.5
  10.2 1.9 %shard_map.101 = (bf16[5,256,256]{2,1,0:T(8,128)(2,1)S(1)}, bf16[1024,256]{1,0:T(8,128)(2,1)S(1)}, bf16[1024,256]{1,0:T(8,128)(2,1)S(1)}, f32[3,256]{1,0:T(4,128...) custom-call(bf16[16,128]{1,0:T(8,128)(2,1)S(1)} %copy-done.2, ...), custom_call_target="tpu_custom_call" | custom-call | tf_op jit(solution)/shard_map/pallas_call | solution.py:411
  12.1 5.3 %all-to-all-done.g_ref = bf16[32,24,128]{2,1,0:T(8,128)(2,1)S(1)} async-done(((bf16[32,24,128]{2,1,0:T(8,128)(2,1)}), bf16[32,24,128]{2,1,0:T(8,128)(2,1)S(1)}, u32[]{:S(2)}, u32[]{:S(2)}) %all-to-all-start) | async-done | bytes 196640 | tf_op jit(solution)/shard_map/all_to_all | solution.py:406
  17.4 10.3 %shard_map.102 = f32[16,128]{1,0:T(8,128)} custom-call(bf16[32,24,128]{2,1,0:T(8,128)(2,1)S(1)} %all-to-all-done.g_ref, f32[16,128]{1,0:T(8,128)S(1)} %get-tuple-element.13.left_ref, bf16[256,512]{1,0:T(8,128)(2,1)S(1)} %get-tuple-element.14.spread_ref, bf16[5,256,256]{2,1,0:T(8,128)(2,1)S(1)} %get-tuple-element.15.w1_ref, ...), custom_call_target="tpu_custom_call" | custom-call | tf_op jit(solution)/shard_map/pallas_call | solution.py:430
Async XLA Ops:
  1.5 8.0 %copy-start = (bf16[9,64,64]{2,1,0:T(8,128)(2,1)S(1)}, bf16[9,64,64]{2,1,0:T(8,128)(2,1)}, u32[]{:S(2)}) copy-start(bf16[9,64,64]{2,1,0:T(8,128)(2,1)} %k2_ref.1) | copy-start | bytes 221188
  1.5 8.0 %copy-start.1 = (bf16[9,64,64]{2,1,0:T(8,128)(2,1)S(1)}, bf16[9,64,64]{2,1,0:T(8,128)(2,1)}, u32[]{:S(2)}) copy-start(bf16[9,64,64]{2,1,0:T(8,128)(2,1)} %k3_ref.1) | copy-start | bytes 221188
  1.5 8.0 %copy-start.6 = (f32[64]{0:T(128)S(1)}, f32[64]{0:T(128)}, u32[]{:S(2)}) copy-start(f32[64]{0:T(128)} %param.17) | copy-start | bytes 772
  1.5 8.1 %copy-start.7 = (s32[1,1,8]{2,1,0:T(1,128)S(1)}, s32[1,1,8]{2,1,0:T(1,128)}, u32[]{:S(2)}) copy-start(s32[1,1,8]{2,1,0:T(1,128)} %param.18) | copy-start | bytes 100
  1.5 15.9 %all-to-all-start = ((bf16[32,24,128]{2,1,0:T(8,128)(2,1)}), bf16[32,24,128]{2,1,0:T(8,128)(2,1)S(1)}, u32[]{:S(2)}, u32[]{:S(2)}) async-start(bf16[32,24,128]{2,1,0:T(8,128)(2,1)} %shard_map.100), calls=%async_computation | async-start | bytes 393216 | tf_op jit(solution)/shard_map/all_to_all | solution.py:406
  8.9 0.7 %copy-start.3 = (f32[64,9]{0,1:T(8,128)S(1)}, f32[64,9]{0,1:T(8,128)}, u32[]{:S(2)}) copy-start(f32[64,9]{0,1:T(8,128)} %param.12) | copy-start | bytes 6916
  9.5 0.7 %copy-start.2 = (bf16[16,128]{1,0:T(8,128)(2,1)S(1)}, bf16[16,128]{1,0:T(8,128)(2,1)}, u32[]{:S(2)}) copy-start(bf16[16,128]{1,0:T(8,128)(2,1)} %left_ref.3) | copy-start | bytes 12292
  9.5 0.7 %copy-start.4 = (f32[64]{0:T(128)S(1)}, f32[64]{0:T(128)}, u32[]{:S(2)}) copy-start(f32[64]{0:T(128)} %param.13) | copy-start | bytes 772
  9.6 0.7 %copy-start.5 = (f32[64]{0:T(128)S(1)}, f32[64]{0:T(128)}, u32[]{:S(2)}) copy-start(f32[64]{0:T(128)} %param.15) | copy-start | bytes 772
